TPU v7x, 256 devices: a whole 4x4x8 slice. The times are simulated.
256 devices in a mesh: replica: 8 (over x, core), fsdp: 16 (over y_lo, z), tensor: 2 (over y_hi).
Axes of the slice: x: 4, y: 4 (y_hi: 2, y_lo: 2; y = y_hi * 2 + y_lo), z: 8, core: 2. Of those that a mesh axis runs over, the one named last changes fastest.
Arguments:
- pseudo_grads: float32 [8, 4096, 5120], P('replica', 'fsdp', 'tensor'), may hold values from -6 to 6
- counts: int32 [8], P('replica'), may hold values from 1024 to 8703, as said below
- master: float32 [4096, 5120], P(('fsdp', 'replica'), 'tensor')
- momentum: float32 [4096, 5120], P(('fsdp', 'replica'), 'tensor'), may hold values from -4 to 4
- tokens: bfloat16 [128, 512, 4096], P(('replica', 'fsdp'), None, 'tensor')
- norm_gain: float32 [4096], replicated, may hold values from 0.1 to 1.9
- lengths: int32 [128], P(('replica', 'fsdp')), may hold values from 128 to 512, as said below
Outputs:
- new_master: float32 [4096, 5120], P(('fsdp', 'replica'), 'tensor')
- new_momentum: float32 [4096, 5120], P(('fsdp', 'replica'), 'tensor')
- context: bfloat16 [128, 512, 4096], P(('replica', 'fsdp'), None, 'tensor')
Inputs may be any that keep to these rules, and one draw needn't show every extreme that they name: `lengths`: live positions of each batch row; later positions are padding, and some row is full. `counts`: tokens each replica processed; both ends of the range are reached.
All inputs are finite; a program needn't handle non-finite values.
Results may differ from a plain program's by a relative error of at most 0.0089.
The roundings to bfloat16 on the way count: a program that leaves them out, or rounds other values in their place, can miss the bound.
Values may be sent and summed in bfloat16 or wider, within the bound.
No kernel may reach another device: no remote copies, remote signals or barrier semaphores. Data moves between devices by JAX's collectives and lax.ppermute only.
A program may use at most 128 MiB of HBM per device.

v0:
```python
import jax
import jax.numpy as jnp
from jax import lax
from jax.sharding import PartitionSpec as P

D = 4096
HD = 128
QPK = 8


outer_momentum = 0.9
outer_rate = 0.7


def normalize(rows, gain):
    values = rows.astype(jnp.float32)
    scale = lax.rsqrt(jnp.mean(values * values, axis=-1, keepdims=True) + 1e-05)
    return (values * scale * gain).astype(jnp.bfloat16)


def rotate(values):
    length = values.shape[1]
    half = HD // 2
    freq = 500000.0 ** (-(jnp.arange(half, dtype=jnp.float32) * 2.0 / HD))
    angle = jnp.arange(length, dtype=jnp.float32)[:, None] * freq[None, :]
    shape = (1, length) + (1,) * (values.ndim - 3) + (half,)
    cosine = jnp.cos(angle).reshape(shape)
    sine = jnp.sin(angle).reshape(shape)
    first = values[..., :half]
    second = values[..., half:]
    return jnp.concatenate(
        [first * cosine - second * sine, second * cosine + first * sine], axis=-1
    )


def attention(proj, lens):
    batch, length, width = proj.shape
    groups = width // ((QPK + 2) * HD)
    parts = proj.reshape(batch, length, groups, QPK + 2, HD)
    query = rotate(parts[:, :, :, :QPK]).astype(jnp.bfloat16)
    keys = rotate(parts[:, :, :, QPK]).astype(jnp.bfloat16)
    values = parts[:, :, :, QPK + 1].astype(jnp.bfloat16)
    scores = jnp.einsum(
        "rsgqh,rtgh->rgqst", query, keys, preferred_element_type=jnp.float32
    ) * HD ** (-0.5)
    position = jnp.arange(length, dtype=jnp.int32)
    causal = (position[None, :] <= position[:, None])[None, None, None]
    inside = position[None, None, None, None, :] < lens.reshape(batch, 1, 1, 1, 1)
    scores = jnp.where(causal & inside, scores, -1e30)
    top = jnp.max(scores, axis=-1, keepdims=True)
    raised = jnp.exp(scores - top)
    probs = (raised / jnp.sum(raised, axis=-1, keepdims=True)).astype(jnp.bfloat16)
    mixed = jnp.einsum("rgqst,rtgh->rsgqh", probs, values, preferred_element_type=jnp.float32)
    live = (position[None, :] < lens[:, None]).reshape(batch, length, 1, 1, 1)
    return (
        jnp.where(live, mixed, 0.0).astype(jnp.bfloat16).reshape(batch, length, groups * QPK * HD)
    )


def per_device(pseudo_grads, counts, master, momentum, tokens, norm_gain, lengths):
    local = pseudo_grads[0]
    count_f = counts.astype(jnp.float32)
    total = lax.psum(count_f[0], "replica")
    summed = lax.psum_scatter(local * count_f[0], "replica", scatter_dimension=0, tiled=True)
    delta = summed / total
    new_momentum = outer_momentum * momentum + delta
    new_master = master - outer_rate * (delta + outer_momentum * new_momentum)
    shard = new_master.astype(jnp.bfloat16)
    rows = lax.all_gather(tokens, "tensor", axis=2, tiled=True)
    batch, length, features = rows.shape
    normed = normalize(rows, norm_gain).reshape(batch * length, features)
    columns = shard.shape[1]
    block = lax.all_gather(shard, "replica", axis=0, tiled=True)
    full = lax.all_gather(block, "fsdp", axis=0, tiled=True)
    proj = jnp.dot(normed, full, preferred_element_type=jnp.float32)
    proj = (proj * D ** (-0.5)).reshape(batch, length, columns)
    context = attention(proj, lengths)
    return (new_master, new_momentum, context)


def solution(mesh):
    in_specs = (
        P("replica", "fsdp", "tensor"),
        P("replica"),
        P(("fsdp", "replica"), "tensor"),
        P(("fsdp", "replica"), "tensor"),
        P(("replica", "fsdp"), None, "tensor"),
        P(),
        P(("replica", "fsdp")),
    )
    out_specs = (
        P(("fsdp", "replica"), "tensor"),
        P(("fsdp", "replica"), "tensor"),
        P(("replica", "fsdp"), None, "tensor"),
    )
    return jax.shard_map(
        per_device, mesh=mesh, in_specs=in_specs, out_specs=out_specs, check_vma=False
    )
```

profile of v0, /device:TPU:1, one launch (start us, length us, event | category | flops | bytes accessed | tf_op | source)
XLA Modules:
  0.0 450.3 jit_solution(2991806084721692770)
XLA Ops:
  7.2 0.0 reduce-scatter.2.cloned.1.call-start
  7.9 3.4 multiply_bitcast_fusion
  11.4 0.0 reduce-scatter.2.cloned.1.call-update
  11.4 0.0 all-gather.6.cloned.1.call-start
  11.4 16.2 %psum.7 = f32[]{:T(128)} all-reduce(f32[]{:T(128)} %bitcast), channel_id=1, replica_groups=mesh['replica'=8,'fsdp'=16,'tensor'=2] {'replica'}, use_global_device_ids=true, to_apply=%region_1.0 | all-reduce | flops 1 | bytes 8 | tf_op jit(solution)/shard_map/psum | solution.py:63
  27.7 22.2 %reduce-scatter.2.cloned.1.call-done = f32[32,2560]{1,0:T(8,128)} async-done(((f32[256,2560]{1,0:T(8,128)}), f32[32,2560]{1,0:T(8,128)}) %reduce-scatter.2.cloned.1.call-update) | async-done | bytes 327696 | tf_op jit(solution)/shard_map/reduce_scatter | solution.py:64
  49.9 2.6 fusion.33
  52.6 0.0 all-gather.6.cloned.1.call-update
  52.6 0.0 copy-start.2
  52.6 0.0 all-gather.4.cloned.1.call-start
  52.6 0.7 all-gather.4.cloned.1.call-update
  53.3 0.0 all-gather.8.cloned.1.call-start
  53.4 27.9 %all-gather.6.cloned.1.call-done = bf16[256,2560]{1,0:T(8,128)(2,1)} async-done(((bf16[32,2560]{1,0:T(8,128)(2,1)}), bf16[256,2560]{1,0:T(8,128)(2,1)}) %all-gather.6.cloned.1.call-update) | async-done | bytes 1310736 | tf_op jit(solution)/shard_map/all_gather | solution.py:73
  81.2 0.0 all-gather.8.cloned.1.call-update
  81.9 0.1 fusion.21
  82.1 1.0 fusion.29
  83.1 62.9 %all-gather.4.cloned.1.call-done = bf16[1,512,4096]{2,1,0:T(8,128)(2,1)} async-done(((bf16[1,512,2048]{2,1,0:T(8,128)(2,1)}), bf16[1,512,4096]{2,1,0:T(8,128)(2,1)}) %all-gather.4.cloned.1.call-update) | async-done | bytes 4194320 | tf_op jit(solution)/shard_map/all_gather | solution.py:69
  146.0 3.1 fusion.2
  149.0 225.4 %all-gather.8.cloned.1.call-done = bf16[4096,2560]{1,0:T(8,128)(2,1)} async-done(((bf16[256,2560]{1,0:T(8,128)(2,1)}), bf16[4096,2560]{1,0:T(8,128)(2,1)}) %all-gather.8.cloned.1.call-update) | async-done | bytes 20971536 | tf_op jit(solution)/shard_map/all_gather | solution.py:74
  374.5 18.1 %convolution_multiply_fusion = f32[512,2560]{1,0:T(8,128)} fusion(bf16[4096,2560]{1,0:T(8,128)(2,1)} %all-gather.8.cloned.1.call-done, bf16[1,512,4096]{2,1,0:T(8,128)(2,1)} %all-gather.4.cloned.1.call-done, f32[4096]{0:T(1024)S(1)} %copy-done.2, f32[512]{0:T(512)S(1)} %add_rsqrt_fusion), kind=kOutput, calls=%fused_computation.13 | convolution fusion | flops 10747117568 | bytes 30427136 | tf_op jit(solution)/shard_map/dot_general | solution.py:75
  392.5 5.9 %copy.16 = f32[512,2560]{0,1:T(8,128)} copy(f32[512,2560]{1,0:T(8,128)} %convolution_multiply_fusion) | data formatting | bytes 10485760 | tf_op jit(solution)/shard_map/mul | solution.py:76
  398.4 4.2 fusion.34
  402.6 1.1 slice.29
  403.7 3.9 copy.27
  407.6 2.8 copy.28
  410.4 0.2 copy.26
  410.6 0.3 fusion.22
  410.8 4.6 %fusion.15 = (bf16[512,2,8,64]{3,0,2,1:T(8,128)(2,1)S(1)}, bf16[512,2,8,64]{3,0,2,1:T(8,128)(2,1)S(1)}) fusion(f32[1,512,2,8,64]{4,1,3,2,0:T(8,128)} %copy.28, f32[1,512,2,8,64]{4,1,3,2,0:T(8,128)} %copy.27, f32[512,64]{1,0:T(8,128)S(1)} %get-tuple-element.19, f32[512,64]{1,0:T(8,128)S(1)} %get-tuple-element.18), kind=kLoop, calls=%fused_computation.22 | loop fusion | flops 4194304 | bytes 6553600 | tf_op jit(solution)/shard_map/concatenate | solution.py:31
  415.5 7.9 %fusion.1 = (f32[2,8,512]{2,1,0:T(8,128)S(1)}, f32[2,512,512,8]{2,1,3,0:T(8,128)}) fusion(pred[512,512]{0,1:T(8,128)(4,1)S(1)} %fusion.21, bf16[512,2,8,64]{3,0,2,1:T(8,128)(2,1)S(1)} %get-tuple-element.13, bf16[512,2,8,64]{3,0,2,1:T(8,128)(2,1)S(1)} %get-tuple-element.12, bf16[512,2,64]{2,0,1:T(8,128)(2,1)S(1)} %get-tuple-element.17, ...), kind=kOutput, calls=%fused_computation.4 | convolution fusion | flops 1091035136 | bytes 19431424 | tf_op jit(solution)/shard_map/rsgqh,rtgh->rgqst/dot_general | solution.py:43
  423.4 9.2 %fusion = f32[2,8,512]{2,1,0:T(8,128)S(1)} fusion(f32[2,512,512,8]{2,1,3,0:T(8,128)} %get-tuple-element.21, f32[2,8,512]{2,1,0:T(8,128)S(1)} %get-tuple-element.20, pred[512,512]{0,1:T(8,128)(4,1)S(1)} %fusion.21), kind=kLoop, calls=%fused_computation.3 | loop fusion | flops 16769024 | bytes 17104896 | tf_op jit(solution)/shard_map/reduce_sum | solution.py:52
  432.6 8.8 %fusion.10 = bf16[1,2,128,8,512]{4,2,3,1,0:T(8,128)(2,1)S(1)} fusion(f32[2,8,512]{2,1,0:T(8,128)S(1)} %fusion, f32[2,8,512]{2,1,0:T(8,128)S(1)} %get-tuple-element.20, f32[2,512,512,8]{2,1,3,0:T(8,128)} %get-tuple-element.21, pred[512,512]{0,1:T(8,128)(4,1)S(1)} %fusion.21, pred[512]{0:T(512)(128)(4,1)S(1)} %iota_compare_fusion.1, ...), kind=kOutput, calls=%fused_computation.16 | convolution fusion | flops 1096810496 | bytes 19464704 | tf_op jit(solution)/shard_map/rgqst,rtgh->rsgqh/dot_general | solution.py:53
  441.4 2.4 copy.22
  (8 shorter events, 0.0 us)
Async XLA Ops:
  7.2 42.8 %copy-start.1 = (f32[32,2560]{1,0:T(8,128)S(1)}, f32[32,2560]{1,0:T(8,128)}, u32[]{:S(2)}) copy-start(f32[32,2560]{1,0:T(8,128)} %param.10) | copy-start | bytes 983044
  7.2 42.8 %copy-start = (f32[32,2560]{1,0:T(8,128)S(1)}, f32[32,2560]{1,0:T(8,128)}, u32[]{:S(2)}) copy-start(f32[32,2560]{1,0:T(8,128)} %param.9) | copy-start | bytes 983044
  7.2 42.7 %reduce-scatter.2.cloned.1.call-start = ((), (), s32[]{:S(2)}) async-start(), calls=%async_computation.1 | async-start | bytes 2949120 | tf_op jit(solution)/shard_map/reduce_scatter | solution.py:64
  11.4 69.8 %all-gather.6.cloned.1.call-start = ((), (), s32[]{:S(2)}) async-start(), calls=%async_computation.3 | async-start | bytes 1474560 | tf_op jit(solution)/shard_map/all_gather | solution.py:73
  52.6 321.9 %copy-start.2 = (f32[4096]{0:T(1024)S(1)}, f32[4096]{0:T(1024)}, u32[]{:S(2)}) copy-start(f32[4096]{0:T(1024)} %param.12) | copy-start | bytes 49156
  52.6 93.4 %all-gather.4.cloned.1.call-start = ((), (), s32[]{:S(2)}) async-start(), calls=%async_computation.2 | async-start | bytes 6291456 | tf_op jit(solution)/shard_map/all_gather | solution.py:69
  53.3 321.1 %all-gather.8.cloned.1.call-start = ((), (), s32[]{:S(2)}) async-start(), calls=%async_computation.4 | async-start | bytes 22282240 | tf_op jit(solution)/shard_map/all_gather | solution.py:74
Sparse Core Ops, SparseCore 0:
  11.5 38.3 reduce-scatter.1
  52.7 28.4 all-gather.5
  83.0 62.8 all-gather.3
  147.6 226.8 all-gather.7
where the time goes:
time: 451 us; the launch traced here: 450 us
  waiting for transfers between devices  339 us (75%)
  matrix products  34.8 us (8%)
  other arithmetic  24.4 us (5%)
  local copies, waits for them, and re-layouts  20.4 us (5%)
  blocking collectives  16.2 us (4%)
  between operations  15.2 us (3%)
    all_gather x1, waiting for transfers between devices, per_device(): full = lax.all_gather(block, 'fsdp', axis=0, tiled=True)  225 us
    all_gather x1, waiting for transfers between devices, per_device(): rows = lax.all_gather(tokens, 'tensor', axis=2, tiled=True)  62.9 us
    all_gather x1, waiting for transfers between devices, per_device(): block = lax.all_gather(shard, 'replica', axis=0, tiled=True)  27.9 us
    reduce_scatter x1, waiting for transfers between devices, per_device(): lax.psum_scatter(local * count_f[0], 'replica', scatter_dimension=0, tile...  22.2 us
    dot_general x1, matrix products, per_device(): proj = jnp.dot(normed, full, preferred_element_type=jnp.float32)  18.1 us
    psum x1, blocking collectives, per_device(): total = lax.psum(count_f[0], 'replica')  16.2 us
    unnamed x10, local copies, waits for them, and re-layouts  9.26 us
    reduce_sum x1, other arithmetic, attention(): jnp.sum(raised, axis=-1, keepdims=True)  9.18 us
  transfers between devices with their start and end apart: 4, of which 4 were waited for; matrix products, arithmetic and copies ran while one was open for 1% of the time, Pallas kernels for 0%

commit v1 on v0

v1 whole, which is shorter than its diff:
```python
import functools

import jax
import jax.numpy as jnp
from jax import lax
from jax.experimental import pallas as pl
from jax.experimental.pallas import tpu as pltpu
from jax.sharding import PartitionSpec as P

D = 4096
HD = 128
QPK = 8
SEQ = 512
GROUP = (QPK + 2) * HD
HALF = D // 2
VMEM_LIMIT = 60 << 20
LOG2E = 1.4426950408889634
AXES = ("replica", "fsdp", "tensor")
NX, NC, NY, NZ = 4, 2, 2, 8

outer_momentum = 0.9
outer_rate = 0.7


def device(x, c, y, z, h):
    return (((x % NX) * NC + c) * NY * NZ + y * NZ + z % NZ) * 2 + h


def places():
    for x in range(NX):
        for c in range(NC):
            for y in range(NY):
                for z in range(NZ):
                    for h in range(2):
                        yield x, c, y, z, h


def pairs(target):
    return [(device(*p), device(*target(*p))) for p in places()]


def send(value, target):
    return lax.ppermute(value, AXES, pairs(target))


def after(value, *others):
    return lax.optimization_barrier((value, *others))[0]


def sibling(x, c, y, z, h):
    return x, 1 - c, y, z, h


def partner(x, c, y, z, h):
    return x, c, y, z, 1 - h


def along_x(step):
    return lambda x, c, y, z, h: (x + step, c, y, z, h)


NEAR = ((2, 0), (1, 0), (3, 0), (2, 1), (1, 1), (3, 1), (0, 1))
NEAR_Z = (4, 3, -3, 2, -2, 1, -1)


def near_target(i):
    def target(x, c, y, z, h):
        if c == 0:
            return x + NEAR[i][0], c, (y + NEAR[i][1]) % NY, z, h
        return x, c, y, z + NEAR_Z[i], h

    return target


def near_gather(own):
    first = [send(own, near_target(i)) for i in range(3)]
    own_later = after(own, *first)
    return [own] + first + [send(own_later, near_target(i)) for i in range(3, 7)]


def far_groups():
    groups = []
    for h in range(2):
        for x in range(NX):
            for y in range(NY):
                groups.append([device(x, 0, y, z, h) for z in range(NZ)])
        for z in range(NZ):
            groups.append([device(x, 1, y, z, h) for y in range(NY) for x in range(NX)])
    return groups


def place_kernel(at_ref, *refs):
    *blocks, out = refs
    for i, block in enumerate(blocks):
        rows = block.shape[0]
        start = pl.multiple_of(at_ref[i], 64)
        out[pl.ds(start, rows), :] = block[...]


def place(at, blocks):
    width = blocks[0].shape[1]
    total = sum(b.shape[0] for b in blocks)
    return pl.pallas_call(
        place_kernel,
        out_shape=jax.ShapeDtypeStruct((total, width), blocks[0].dtype),
        grid_spec=pltpu.PrefetchScalarGridSpec(
            num_scalar_prefetch=1,
            grid=(1,),
            in_specs=[pl.BlockSpec(b.shape, lambda i, at: (0, 0)) for b in blocks],
            out_specs=pl.BlockSpec((total, width), lambda i, at: (0, 0)),
        ),
        compiler_params=pltpu.CompilerParams(vmem_limit_bytes=VMEM_LIMIT),
        cost_estimate=pl.CostEstimate(
            flops=0, transcendentals=0, bytes_accessed=4 * total * width
        ),
        name="place",
    )(at, *blocks)


def norm_kernel(high_ref, own, other, gain, out):
    first, second = own[...].astype(jnp.float32), other[...].astype(jnp.float32)
    square = jnp.sum(first * first + second * second, axis=-1, keepdims=True)
    scale = lax.rsqrt(square * (1.0 / D) + 1e-05)
    keep = high_ref[0] == 0
    for a, b, start in ((first, second, 0), (second, first, HALF)):
        values = jnp.where(keep, a, b) * scale * gain[:, start : start + HALF]
        out[:, start : start + HALF] = values.astype(jnp.bfloat16)


def normalize(high, own, other, gain):
    tile = 64
    count = own.shape[0]
    rows = pl.BlockSpec((tile, HALF), lambda i, w: (i, 0))
    return pl.pallas_call(
        norm_kernel,
        out_shape=jax.ShapeDtypeStruct((count, D), jnp.bfloat16),
        grid_spec=pltpu.PrefetchScalarGridSpec(
            num_scalar_prefetch=1,
            grid=(count // tile,),
            in_specs=[rows, rows, pl.BlockSpec((1, D), lambda i, w: (0, 0))],
            out_specs=pl.BlockSpec((tile, D), lambda i, w: (i, 0)),
        ),
        compiler_params=pltpu.CompilerParams(vmem_limit_bytes=VMEM_LIMIT),
        cost_estimate=pl.CostEstimate(
            flops=8 * count * D, transcendentals=0, bytes_accessed=4 * count * D
        ),
        name="normalize",
    )(high, own, other, gain.reshape(1, D))


def project_kernel(
    core_ref, own_low, own_high, sib_low, sib_high, by_z, by_plane, out, rows
):
    for i, (low, high) in enumerate(((own_low, own_high), (sib_low, sib_high))):
        rows[i * SEQ : (i + 1) * SEQ, :512] = low[...]
        rows[i * SEQ : (i + 1) * SEQ, 512:] = high[...]

    def add(weights):
        part = jnp.dot(rows[...], weights, preferred_element_type=jnp.float32)
        part = part.reshape(out.shape)

        @pl.when(pl.program_id(0) == 0)
        def _():
            out[...] = part

        @pl.when(pl.program_id(0) > 0)
        def _():
            out[...] += part

    @pl.when(core_ref[0] == 0)
    def _():
        add(jnp.concatenate([by_z[i * 256 : (i + 1) * 256] for i in (0, 2, 1, 3)]))

    @pl.when(core_ref[0] == 1)
    def _():
        add(
            jnp.concatenate(
                [
                    by_plane[y, :, z].reshape(256, by_plane.shape[-1])
                    for y in range(NY)
                    for z in range(2)
                ]
            )
        )


def project(core, normed, weights):
    width = weights.shape[1]
    steps = NZ // 2
    low = pl.BlockSpec((SEQ, 512), lambda t, core: (0, t))
    high = pl.BlockSpec((SEQ, 512), lambda t, core: (0, steps + t))
    shape = (2, SEQ, width)
    own, sib = normed
    return pl.pallas_call(
        project_kernel,
        out_shape=jax.ShapeDtypeStruct(shape, jnp.float32),
        grid_spec=pltpu.PrefetchScalarGridSpec(
            num_scalar_prefetch=1,
            grid=(steps,),
            in_specs=[low, high, low, high]
            + [
                pl.BlockSpec((1024, width), lambda t, core: (jnp.where(core[0] == 0, t, 0), 0)),
                pl.BlockSpec(
                    (NY, NX, 2, 64, width),
                    lambda t, core: (0, 0, jnp.where(core[0] == 0, 0, t), 0, 0),
                ),
            ],
            out_specs=pl.BlockSpec(shape, lambda t, core: (0, 0, 0)),
            scratch_shapes=[pltpu.VMEM((2 * SEQ, 1024), jnp.bfloat16)],
        ),
        compiler_params=pltpu.CompilerParams(vmem_limit_bytes=VMEM_LIMIT),
        cost_estimate=pl.CostEstimate(
            flops=4 * SEQ * D * width,
            transcendentals=0,
            bytes_accessed=2 * D * width + 4 * SEQ * D + 8 * SEQ * width,
        ),
        name="project",
    )(core, own, own, sib, sib, weights, weights.reshape(NY, NX, NZ, 64, width))


def turn(values, cosine, sine):
    return values * cosine + pltpu.roll(values, HD // 2, 1) * sine


def attend_kernel(at_ref, q_ref, kv_ref, cos_ref, sin_ref, mine, theirs, key, value):
    row = pl.program_id(0)
    length = at_ref[row]
    cosine, sine = cos_ref[...], sin_ref[...]
    unit = D**-0.5
    tile = 256

    @pl.when(pl.program_id(1) == 0)
    def _():
        key[...] = turn(kv_ref[0, :, :HD] * unit, cosine, sine).astype(jnp.bfloat16)
        value[...] = (kv_ref[0, :, HD:] * unit).astype(jnp.bfloat16)

    s = lax.broadcasted_iota(jnp.int32, (tile, tile), 0)
    t = lax.broadcasted_iota(jnp.int32, (tile, tile), 1)
    heads = range(2)
    queries = [
        turn(q_ref[0, :, h * HD : (h + 1) * HD] * unit, cosine, sine).astype(jnp.bfloat16)
        for h in heads
    ]
    results = {}
    for block in range(SEQ // tile):
        start, reach = block * tile, (block + 1) * tile
        allowed = [jnp.where((t <= s) & (t + start < length), 0.0, -1e30)]
        if block:
            allowed.insert(0, jnp.where(t < length, 0.0, -1e30))
        live = lax.broadcasted_iota(jnp.int32, (tile, HD), 0) + start < length
        scores = lax.dot_general(
            jnp.concatenate([q[start:reach] for q in queries], axis=0),
            key[:reach],
            (((1,), (1,)), ((), ())),
            preferred_element_type=jnp.float32,
        )
        mask = jnp.concatenate(allowed, axis=1)
        scores = scores.reshape(len(heads), tile, reach) * (HD ** (-0.5) * LOG2E) + mask[None]
        scores = scores.reshape(len(heads) * tile, reach)
        raised = jnp.exp2(scores - jnp.max(scores, axis=1, keepdims=True))
        scale = 1.0 / jnp.sum(raised, axis=1, keepdims=True)
        mixed = jnp.dot(
            raised.astype(jnp.bfloat16), value[:reach], preferred_element_type=jnp.float32
        )
        mixed = mixed * scale
        for h in heads:
            results[start, h * HD] = jnp.where(
                live, mixed[h * tile : (h + 1) * tile], 0.0
            ).astype(jnp.bfloat16)

    def fill(out):
        for (start, column), part in results.items():
            out[start : start + tile, column : column + HD] = part

    pl.when(row == 0)(lambda: fill(mine))
    pl.when(row == 1)(lambda: fill(theirs))


def attend(lens, column, proj, cosine, sine):
    width = QPK * HD
    count = width // (2 * HD)
    at = jnp.concatenate([lens, jnp.reshape(column // (2 * HD), (1,))])
    return pl.pallas_call(
        attend_kernel,
        out_shape=(
            jax.ShapeDtypeStruct((SEQ, 2 * width), jnp.bfloat16),
            jax.ShapeDtypeStruct((SEQ, width), jnp.bfloat16),
        ),
        grid_spec=pltpu.PrefetchScalarGridSpec(
            num_scalar_prefetch=1,
            grid=(2, count),
            in_specs=[
                pl.BlockSpec((1, SEQ, 2 * HD), lambda r, j, at: (r, 0, j)),
                pl.BlockSpec((1, SEQ, 2 * HD), lambda r, j, at: (r, 0, count)),
                pl.BlockSpec((SEQ, HD), lambda r, j, at: (0, 0)),
                pl.BlockSpec((SEQ, HD), lambda r, j, at: (0, 0)),
            ],
            out_specs=(
                pl.BlockSpec(
                    (SEQ, 2 * HD), lambda r, j, at: (0, at[2] + jnp.where(r == 0, j, count - 1))
                ),
                pl.BlockSpec((SEQ, 2 * HD), lambda r, j, at: (0, jnp.where(r == 0, 0, j))),
            ),
            scratch_shapes=[
                pltpu.VMEM((SEQ, HD), jnp.bfloat16),
                pltpu.VMEM((SEQ, HD), jnp.bfloat16),
            ],
        ),
        compiler_params=pltpu.CompilerParams(vmem_limit_bytes=VMEM_LIMIT),
        cost_estimate=pl.CostEstimate(
            flops=8 * SEQ * SEQ * width,
            transcendentals=2 * SEQ * SEQ * width // HD,
            bytes_accessed=12 * SEQ * width,
        ),
        name="attend",
    )(at, proj, proj, cosine, sine)


def insert_kernel(at_ref, part, _, out):
    out[...] = part[...]


def insert(column, part, context):
    width = 2 * HD
    return pl.pallas_call(
        insert_kernel,
        out_shape=jax.ShapeDtypeStruct(context.shape, context.dtype),
        grid_spec=pltpu.PrefetchScalarGridSpec(
            num_scalar_prefetch=1,
            grid=(part.shape[1] // width,),
            in_specs=[
                pl.BlockSpec((SEQ, width), lambda j, at: (0, j)),
                pl.BlockSpec(memory_space=pl.ANY),
            ],
            out_specs=pl.BlockSpec((SEQ, width), lambda j, at: (0, at[0] + j)),
        ),
        input_output_aliases={2: 0},
        compiler_params=pltpu.CompilerParams(vmem_limit_bytes=VMEM_LIMIT),
        cost_estimate=pl.CostEstimate(
            flops=0, transcendentals=0, bytes_accessed=4 * SEQ * part.shape[1]
        ),
        name="insert",
    )(jnp.reshape(column // width, (1,)), part, context)


def per_device(pseudo_grads, counts, master, momentum, tokens, norm_gain, lengths):
    replica, fsdp = lax.axis_index("replica"), lax.axis_index("fsdp")
    x, core = replica // NC, replica % NC
    y, z = fsdp // NZ, fsdp % NZ
    cycle = jnp.where(y == 0, x, 7 - x)

    weight = counts[0].astype(jnp.float32)

    half = HD // 2
    freq = 500000.0 ** (-(jnp.arange(half, dtype=jnp.float32) * 2.0 / HD))
    angle = jnp.arange(SEQ, dtype=jnp.float32)[:, None] * freq[None, :]
    cosine, sine = jnp.cos(angle), jnp.sin(angle)
    cosine = jnp.concatenate([cosine, cosine], axis=1)
    sine = jnp.concatenate([-sine, sine], axis=1)

    def mine(array):
        return lax.dynamic_slice_in_dim(array, core * GROUP, GROUP, axis=1)

    def theirs(array):
        return lax.dynamic_slice_in_dim(array, (1 - core) * GROUP, GROUP, axis=1)

    grads = pseudo_grads[0]
    own_tokens = tokens[0]
    other_tokens = send(own_tokens, partner)


    counted = jnp.broadcast_to(weight, (8, GROUP))
    got = send(jnp.concatenate([theirs(grads) * weight, counted]), sibling)
    states = send(
        after(
            jnp.concatenate(
                [
                    theirs(master),
                    theirs(momentum),
                    jnp.broadcast_to(lengths[0].astype(jnp.float32), (8, GROUP)),
                ]
            ),
            got,
        ),
        sibling,
    )
    lens = jnp.stack([lengths[0], states[64, 0].astype(jnp.int32)])

    places_at = [jnp.where(core == 0, y * NX + x, z)]
    for (dx, dy), dz in zip(NEAR, NEAR_Z):
        plane = (y + NY - dy) % NY * NX + (x + NX - dx) % NX
        places_at.append(jnp.where(core == 0, plane, (z + NZ - dz) % NZ))
    places_at = (jnp.stack(places_at) * 64).astype(jnp.int32)

    summed = mine(grads) * weight + got[:256]
    part = summed.reshape(NX, 64, GROUP)

    def block(step):
        value = lax.dynamic_index_in_dim(part, (x + step) % NX, 0, keepdims=False)
        return jnp.concatenate([value, counted + got[256:]])

    arrived = [send(block(step), along_x(step)) for step in (1, 3, 2)]
    summed = block(0) + arrived[0] + arrived[1] + arrived[2]
    delta = summed[:64] / summed[64, 0]
    pair = []
    for array, kept in ((master, states[:32]), (momentum, states[32:64])):
        a, b = mine(array), kept
        pair.append(
            jnp.concatenate([jnp.where(core == 0, a, b), jnp.where(core == 0, b, a)], axis=0)
        )
    new_momentum = outer_momentum * pair[1] + delta
    new_master = pair[0] - outer_rate * (delta + outer_momentum * new_momentum)
    near = near_gather(new_master.astype(jnp.bfloat16))
    near[0] = after(near[0], other_tokens)
    whole = place(places_at, near)

    def in_order(own, other):
        return jnp.concatenate(
            [jnp.where(core == 0, own, other), jnp.where(core == 0, other, own)], axis=1
        )

    both = (new_master, new_momentum)
    back = send(
        after(
            jnp.concatenate([jnp.where(core == 0, v[32:], v[:32]) for v in both], axis=0),
            whole,
        ),
        sibling,
    )
    outs = [
        in_order(jnp.where(core == 0, v[:32], v[32:]), back[32 * i : 32 * (i + 1)])
        for i, v in enumerate(both)
    ]

    core_id = jnp.reshape(core, (1,)).astype(jnp.int32)
    high_id = jnp.reshape(lax.axis_index("tensor"), (1,)).astype(jnp.int32)
    full = lax.all_gather(whole, AXES, axis=0, tiled=True, axis_index_groups=far_groups())
    kept = normalize(high_id, own_tokens, after(other_tokens, whole), norm_gain)
    normed = (kept, send(kept, sibling))

    full, *outs = lax.optimization_barrier((full, *outs))
    proj = project(core_id, normed, full)
    context, given = attend(lens, core * QPK * HD, proj, cosine, sine)
    context = insert((1 - core) * QPK * HD, send(given, sibling), context)
    return outs[0], outs[1], context[None]


def solution(mesh):
    in_specs = (
        P("replica", "fsdp", "tensor"),
        P("replica"),
        P(("fsdp", "replica"), "tensor"),
        P(("fsdp", "replica"), "tensor"),
        P(("replica", "fsdp"), None, "tensor"),
        P(),
        P(("replica", "fsdp")),
    )
    out_specs = (
        P(("fsdp", "replica"), "tensor"),
        P(("fsdp", "replica"), "tensor"),
        P(("replica", "fsdp"), None, "tensor"),
    )
    return jax.shard_map(
        per_device, mesh=mesh, in_specs=in_specs, out_specs=out_specs, check_vma=False
    )
```

time: 451 us -> 187 us (0.41)
  waiting for transfers between devices: 339 us -> 80.6 us
  Pallas kernels: 0 us -> 46.6 us
  matrix products: 34.8 us -> 0 us
  starting transfers between devices: 0.16 us -> 27.4 us
  blocking collectives: 16.2 us -> 0 us
  local copies, waits for them, and re-layouts: 20.4 us -> 5.55 us
  other arithmetic: 24.4 us -> 9.73 us
    all_gather x3 -> x1, waiting for transfers between devices: 316 us -> 49.3 us  [per_device(): lax.all_gather(whole, AXES, axis=0, tiled=True, axis_index_groups=far_gro...]
    pallas_call x0 -> x5, Pallas kernels: none -> 46.6 us  [the longest x1 19.7 us: project(): pl.pallas_call(project_kernel, out_shape=jax.ShapeDtypeStruct(shape, jnp....]
    dot_general x3 -> x0, matrix products: 34.8 us -> none  [the longest x1 18.1 us: per_device(): proj = jnp.dot(normed, full, preferred_element_type=jnp.float32)]
    ppermute x0 -> x16, waiting for transfers between devices: none -> 31.2 us  [send(): return lax.ppermute(value, AXES, pairs(target))]
    ppermute x0 -> x16, starting transfers between devices: none -> 27.4 us  [send(): return lax.ppermute(value, AXES, pairs(target))]
    reduce_scatter x1 -> x0, waiting for transfers between devices: 22.2 us -> none  [per_device(): lax.psum_scatter(local * count_f[0], 'replica', scatter_dimension=0, tile...]
    psum x1 -> x0, blocking collectives: 16.2 us -> none  [per_device(): total = lax.psum(count_f[0], 'replica')]
    reduce_sum x2 -> x0, other arithmetic: 12.3 us -> none  [the longest x1 9.18 us: attention(): jnp.sum(raised, axis=-1, keepdims=True)]
  transfers between devices with their start and end apart: 4 -> 17, of which waited for: 4 -> 10; matrix products, arithmetic and copies ran while one was open for 1% -> 6% of each run, Pallas kernels for 0% -> 4%
where the time goes in v1:
time: 187 us; the launch traced here: 186 us
  waiting for transfers between devices  80.6 us (43%)
  Pallas kernels  46.6 us (25%)
  starting transfers between devices  27.4 us (15%)
  between operations  16.3 us (9%)
  other arithmetic  9.73 us (5%)
  local copies, waits for them, and re-layouts  5.55 us (3%)
    all_gather x1, waiting for transfers between devices, per_device(): lax.all_gather(whole, AXES, axis=0, tiled=True, axis_index_groups=far_gro...  49.3 us
    ppermute x16, waiting for transfers between devices, send(): return lax.ppermute(value, AXES, pairs(target))  31.2 us
    ppermute x16, starting transfers between devices, send(): return lax.ppermute(value, AXES, pairs(target))  27.4 us
    pallas_call x1, Pallas kernels, project(): pl.pallas_call(project_kernel, out_shape=jax.ShapeDtypeStruct(shape, jnp....  19.7 us
    pallas_call x1, Pallas kernels, attend(): pl.pallas_call(attend_kernel, out_shape=(jax.ShapeDtypeStruct((SEQ, 2 * w...  12.8 us
    pallas_call x1, Pallas kernels, normalize(): pl.pallas_call(norm_kernel, out_shape=jax.ShapeDtypeStruct((count, D), jn...  7.57 us
  transfers between devices with their start and end apart: 17, of which 10 were waited for; matrix products, arithmetic and copies ran while one was open for 6% of the time, Pallas kernels for 4%

profile of v1, /device:TPU:1, one launch (start us, length us, event | category | flops | bytes accessed | tf_op | source)
XLA Modules:
  0.0 186.2 jit_solution(3144381691886627226)
XLA Ops:
  7.9 1.5 multiply_bitcast_fusion
  9.4 1.2 concatenate.43
  10.5 3.2 %collective-permute-start = (f32[264,1280]{1,0:T(8,128)}, f32[264,1280]{1,0:T(8,128)}, u32[]{:S(2)}, u32[]{:S(2)}) collective-permute-start(f32[264,1280]{1,0:T(8,128)} %concatenate.43), channel_id=1, source_target_pairs={{0,32},{1,33},{2,34},{3,35},{4,36},{5,37},{6,38},{7,39},{8,40},{9,... | collective-permute-start | bytes 4055048 | tf_op jit(solution)/shard_map/ppermute | solution.py:43
  13.8 1.2 collective-permute-start.5
  15.8 1.1 collective-permute-done
  16.8 1.5 slice_add_fusion
  19.4 1.8 collective-permute-start.4
  22.7 1.1 collective-permute-start.1
  23.9 7.1 %collective-permute-done.4 = f32[72,1280]{1,0:T(8,128)S(1)} collective-permute-done((f32[72,1280]{1,0:T(8,128)S(1)}, f32[72,1280]{1,0:T(8,128)S(1)}, u32[]{:S(2)}, u32[]{:S(2)}) %collective-permute-start.4) | collective-permute-done | bytes 368672 | tf_op jit(solution)/shard_map/ppermute | solution.py:43
  31.0 7.0 %collective-permute-done.3 = f32[72,1280]{1,0:T(8,128)S(1)} collective-permute-done((f32[72,1280]{1,0:T(8,128)S(1)}, f32[72,1280]{1,0:T(8,128)S(1)}, u32[]{:S(2)}, u32[]{:S(2)}) %collective-permute-start.3) | collective-permute-done | bytes 368672 | tf_op jit(solution)/shard_map/ppermute | solution.py:43
  38.0 1.5 collective-permute-done.2
  41.0 5.9 %collective-permute-start.6 = (bf16[64,1280]{1,0:T(8,128)(2,1)S(1)}, bf16[64,1280]{1,0:T(8,128)(2,1)S(1)}, u32[]{:S(2)}, u32[]{:S(2)}) collective-permute-start(bf16[64,1280]{1,0:T(8,128)(2,1)S(1)} %get-tuple-element.15.refs_0_), channel_id=1, source_target_pairs={{0,128},{1,129},{2,130},{3,131},{4,132},{5,133},{6,134},{7,135},{8... | collective-permute-start | bytes 491528 | tf_op jit(solution)/shard_map/ppermute | solution.py:43
  46.9 1.6 collective-permute-start.7
  48.5 2.8 %collective-permute-start.8 = (bf16[64,1280]{1,0:T(8,128)(2,1)S(1)}, bf16[64,1280]{1,0:T(8,128)(2,1)S(1)}, u32[]{:S(2)}, u32[]{:S(2)}) collective-permute-start(bf16[64,1280]{1,0:T(8,128)(2,1)S(1)} %get-tuple-element.15.refs_0_), channel_id=1, source_target_pairs={{0,192},{1,193},{2,194},{3,195},{4,196},{5,197},{6,198},{7,199},{8... | collective-permute-start | bytes 491528 | tf_op jit(solution)/shard_map/ppermute | solution.py:43
  51.5 5.8 %collective-permute-done.7.refs_2_ = bf16[64,1280]{1,0:T(8,128)(2,1)S(1)} collective-permute-done((bf16[64,1280]{1,0:T(8,128)(2,1)S(1)}, bf16[64,1280]{1,0:T(8,128)(2,1)S(1)}, u32[]{:S(2)}, u32[]{:S(2)}) %collective-permute-start.7) | collective-permute-done | bytes 163872 | tf_op jit(solution)/shard_map/ppermute | solution.py:43
  57.3 1.2 collective-permute-done.8.refs_3_
  58.5 3.6 %collective-permute-start.10 = (bf16[64,1280]{1,0:T(8,128)(2,1)S(1)}, bf16[64,1280]{1,0:T(8,128)(2,1)S(1)}, u32[]{:S(2)}, u32[]{:S(2)}) collective-permute-start(bf16[64,1280]{1,0:T(8,128)(2,1)S(1)} %get-tuple-element.15.refs_0_), channel_id=1, source_target_pairs={{0,80},{1,81},{2,82},{3,83},{4,84},{5,85},{6,86},{7,87},{8,88},{9,... | collective-permute-start | bytes 491528 | tf_op jit(solution)/shard_map/ppermute | solution.py:43
  62.1 2.7 %collective-permute-start.12 = (bf16[64,1280]{1,0:T(8,128)(2,1)S(1)}, bf16[64,1280]{1,0:T(8,128)(2,1)S(1)}, u32[]{:S(2)}, u32[]{:S(2)}) collective-permute-start(bf16[64,1280]{1,0:T(8,128)(2,1)S(1)} %get-tuple-element.15.refs_0_), channel_id=1, source_target_pairs={{0,16},{1,17},{2,18},{3,19},{4,20},{5,21},{6,22},{7,23},{8,24},{9,... | collective-permute-start | bytes 491528 | tf_op jit(solution)/shard_map/ppermute | solution.py:43
  65.3 2.9 %collective-permute-done.5.other = bf16[512,2048]{1,0:T(8,128)(2,1)} collective-permute-done((bf16[512,2048]{1,0:T(8,128)(2,1)}, bf16[512,2048]{1,0:T(8,128)(2,1)}, u32[]{:S(2)}, u32[]{:S(2)}) %collective-permute-start.5) | collective-permute-done | bytes 2097184 | tf_op jit(solution)/shard_map/ppermute | solution.py:43
  69.6 3.2 %place.1 = bf16[512,1280]{1,0:T(8,128)(2,1)} custom-call(s32[8]{0:T(128)} %broadcast_multiply_fusion.at_ref, bf16[64,1280]{1,0:T(8,128)(2,1)} %copy-done.2, bf16[64,1280]{1,0:T(8,128)(2,1)} %copy-done.7, bf16[64,1280]{1,0:T(8,128)(2,1)} %copy-done.8, bf16[64,1280]{1,0:T(8,128)(2,1)} %copy-done.9, bf16[64,1280]{1,0:T(8,128)(2,1)} %copy-done.10, ...), custom_call_target="tpu_custom_call" | custom-call | bytes 2621440 | tf_op jit(solution)/shard_map/place/pallas_call | solution.py:103
  72.8 7.6 %normalize.1.own_low.own_high = bf16[512,4096]{1,0:T(8,128)(2,1)} custom-call(s32[1]{0:T(128)} %bitcast.23.high_ref, bf16[512,2048]{1,0:T(8,128)(2,1)} %bitcast.18.own, bf16[512,2048]{1,0:T(8,128)(2,1)} %collective-permute-done.5.other, f32[1,4096]{1,0:T(1,128)} %bitcast.36), custom_call_target="tpu_custom_call" | custom-call | flops 16777216 | bytes 8388608 | tf_op jit(solution)/shard_map/normalize/pallas_call | solution.py:134
  81.5 1.0 fusion.6
  82.5 1.1 pad_maximum_fusion.7
  83.6 1.2 slice.71
  86.1 2.2 %collective-permute-done.13 = f32[64,1280]{1,0:T(8,128)S(1)} collective-permute-done((f32[64,1280]{1,0:T(8,128)S(1)}, f32[64,1280]{1,0:T(8,128)S(1)}, u32[]{:S(2)}, u32[]{:S(2)}) %collective-permute-start.13) | collective-permute-done | bytes 327712 | tf_op jit(solution)/shard_map/ppermute | solution.py:43
  89.8 49.3 %all-gather.2.cloned.1.call-done.by_z = bf16[4096,1280]{1,0:T(8,128)(2,1)} async-done(((bf16[512,1280]{1,0:T(8,128)(2,1)}), bf16[4096,1280]{1,0:T(8,128)(2,1)}) %all-gather.2.cloned.1.call-update) | async-done | bytes 10485776 | tf_op jit(solution)/shard_map/all_gather | solution.py:437
  139.2 19.7 %project.1.q_ref.kv_ref = f32[2,512,1280]{2,1,0:T(8,128)} custom-call(s32[1]{0:T(128)} %bitcast.22.core_ref, bf16[512,4096]{1,0:T(8,128)(2,1)} %normalize.1.own_low.own_high, bf16[512,4096]{1,0:T(8,128)(2,1)} %normalize.1.own_low.own_high, bf16[512,4096]{1,0:T(8,128)(2,1)} %collective-permute-done.14.sib_low.sib_high, ...), custom_call_target="tpu_custom_call" | custom-call | flops 10737418240 | bytes 24117248 | tf_op jit(solution)/shard_map/project/pallas_call | solution.py:194
  158.8 12.8 %attend.1 = (bf16[512,2048]{1,0:T(8,128)(2,1)}, bf16[512,1024]{1,0:T(8,128)(2,1)}) custom-call(s32[3]{0:T(128)} %pad_add_fusion.at_ref, f32[2,512,1280]{2,1,0:T(8,128)} %project.1.q_ref.kv_ref, f32[2,512,1280]{2,1,0:T(8,128)} %project.1.q_ref.kv_ref, f32[512,128]{1,0:T(8,128)} %get-tuple-element.50.cos_ref, f32[512,128]{1,0:T(8,128)} %get-tuple-element.51.sin_ref), custom_call_target="tpu_custom_call" | custom-call | flops 2147483648 | bytes 6291456 | tf_op jit(solution)/shard_map/attend/pallas_call | solution.py:283
  171.6 0.9 collective-permute-start.15
  172.5 2.5 %collective-permute-done.15.part = bf16[512,1024]{1,0:T(8,128)(2,1)S(1)} collective-permute-done((bf16[512,1024]{1,0:T(8,128)(2,1)}, bf16[512,1024]{1,0:T(8,128)(2,1)S(1)}, u32[]{:S(2)}, u32[]{:S(2)}) %collective-permute-start.15) | collective-permute-done | bytes 1048608 | tf_op jit(solution)/shard_map/ppermute | solution.py:43
  175.0 1.0 copy-done.1
  176.0 3.4 %insert.1 = bf16[512,2048]{1,0:T(8,128)(2,1)} custom-call(s32[1]{0:T(128)} %bitcast.19.at_ref, bf16[512,1024]{1,0:T(8,128)(2,1)} %copy-done.1, bf16[512,2048]{1,0:T(8,128)(2,1)} %get-tuple-element.22._), custom_call_target="tpu_custom_call", output_to_operand_aliasing={{}: (2, {})} | custom-call | bytes 2097152 | tf_op jit(solution)/shard_map/insert/pallas_call | solution.py:325
  (63 shorter events, 9.5 us)
Async XLA Ops:
  7.2 132.0 %all-gather.2.cloned.1.call-start = ((), (), s32[]{:S(2)}) async-start(), calls=%async_computation | async-start | bytes 11796480 | tf_op jit(solution)/shard_map/all_gather | solution.py:437
  7.9 7.8 %copy-start.3 = (f32[32,2560]{1,0:T(8,128)S(1)}, f32[32,2560]{1,0:T(8,128)}, u32[]{:S(2)}) copy-start(f32[32,2560]{1,0:T(8,128)} %param.10) | copy-start | bytes 983044
  9.3 6.4 %copy-start.4 = (f32[32,2560]{1,0:T(8,128)S(1)}, f32[32,2560]{1,0:T(8,128)}, u32[]{:S(2)}) copy-start(f32[32,2560]{1,0:T(8,128)} %param.9) | copy-start | bytes 983044
  9.4 7.5 %copy-start = (f32[1,256,2560]{2,1,0:T(8,128)S(1)}, f32[1,256,2560]{2,1,0:T(8,128)}, u32[]{:S(2)}) copy-start(f32[1,256,2560]{2,1,0:T(8,128)} %param.7) | copy-start | bytes 7864324
  10.5 6.3 %collective-permute-start = (f32[264,1280]{1,0:T(8,128)}, f32[264,1280]{1,0:T(8,128)}, u32[]{:S(2)}, u32[]{:S(2)}) collective-permute-start(f32[264,1280]{1,0:T(8,128)} %concatenate.43), channel_id=1, source_target_pairs={{0,32},{1,33},{2,34},{3,35},{4,36},{5,37},{6,38},{7,39},{8,40},{9,... | collective-permute-start | bytes 4055048 | tf_op jit(solution)/shard_map/ppermute | solution.py:43
  13.8 54.3 %collective-permute-start.5 = (bf16[512,2048]{1,0:T(8,128)(2,1)}, bf16[512,2048]{1,0:T(8,128)(2,1)}, u32[]{:S(2)}, u32[]{:S(2)}) collective-permute-start(bf16[512,2048]{1,0:T(8,128)(2,1)} %bitcast.18.own), channel_id=1, source_target_pairs={{0,1},{1,0},{2,3},{3,2},{4,5},{5,4},{6,7},{7,6},{8,9},{9,8},{10,11... | collective-permute-start | bytes 6291464 | tf_op jit(solution)/shard_map/ppermute | solution.py:43
  19.4 11.6 %collective-permute-start.4 = (f32[72,1280]{1,0:T(8,128)S(1)}, f32[72,1280]{1,0:T(8,128)S(1)}, u32[]{:S(2)}, u32[]{:S(2)}) collective-permute-start(f32[72,1280]{1,0:T(8,128)S(1)} %get-tuple-element.44), channel_id=1, source_target_pairs={{0,128},{1,129},{2,130},{3,131},{4,132},{5,133},{6,134},{7,135},{8... | collective-permute-start | bytes 1105928 | tf_op jit(solution)/shard_map/ppermute | solution.py:43
  21.1 16.9 %collective-permute-start.3 = (f32[72,1280]{1,0:T(8,128)S(1)}, f32[72,1280]{1,0:T(8,128)S(1)}, u32[]{:S(2)}, u32[]{:S(2)}) collective-permute-start(f32[72,1280]{1,0:T(8,128)S(1)} %get-tuple-element.43), channel_id=1, source_target_pairs={{0,192},{1,193},{2,194},{3,195},{4,196},{5,197},{6,198},{7,199},{8... | collective-permute-start | bytes 1105928 | tf_op jit(solution)/shard_map/ppermute | solution.py:43
  22.0 17.5 %collective-permute-start.2 = (f32[72,1280]{1,0:T(8,128)S(1)}, f32[72,1280]{1,0:T(8,128)S(1)}, u32[]{:S(2)}, u32[]{:S(2)}) collective-permute-start(f32[72,1280]{1,0:T(8,128)S(1)} %get-tuple-element.42), channel_id=1, source_target_pairs={{0,64},{1,65},{2,66},{3,67},{4,68},{5,69},{6,70},{7,71},{8,72},{9,... | collective-permute-start | bytes 1105928 | tf_op jit(solution)/shard_map/ppermute | solution.py:43
  22.7 17.4 %copy-start.5 = (f32[32,2560]{1,0:T(8,128)S(1)}, f32[32,2560]{1,0:T(8,128)}, u32[]{:S(2)}) copy-start(f32[32,2560]{1,0:T(8,128)} %param.9) | copy-start | bytes 983044
  22.7 17.4 %collective-permute-start.1 = (f32[72,1280]{1,0:T(8,128)S(1)}, f32[72,1280]{1,0:T(8,128)S(1)}, u32[]{:S(2)}, u32[]{:S(2)}) collective-permute-start(f32[72,1280]{1,0:T(8,128)S(1)} %maximum_maximum_fusion), channel_id=1, source_target_pairs={{0,32},{1,33},{2,34},{3,35},{4,36},{5,37},{6,38},{7,39},{8,40},{9,... | collective-permute-start | bytes 1105928 | tf_op jit(solution)/shard_map/ppermute | solution.py:43
  40.1 0.8 copy-start.6
  40.9 27.2 %copy-start.2 = (bf16[64,1280]{1,0:T(8,128)(2,1)}, bf16[64,1280]{1,0:T(8,128)(2,1)S(1)}, u32[]{:S(2)}) copy-start(bf16[64,1280]{1,0:T(8,128)(2,1)S(1)} %get-tuple-element.15.refs_0_) | copy-start | bytes 491524
  41.0 10.5 %collective-permute-start.6 = (bf16[64,1280]{1,0:T(8,128)(2,1)S(1)}, bf16[64,1280]{1,0:T(8,128)(2,1)S(1)}, u32[]{:S(2)}, u32[]{:S(2)}) collective-permute-start(bf16[64,1280]{1,0:T(8,128)(2,1)S(1)} %get-tuple-element.15.refs_0_), channel_id=1, source_target_pairs={{0,128},{1,129},{2,130},{3,131},{4,132},{5,133},{6,134},{7,135},{8... | collective-permute-start | bytes 491528 | tf_op jit(solution)/shard_map/ppermute | solution.py:43
  46.9 10.4 %collective-permute-start.7 = (bf16[64,1280]{1,0:T(8,128)(2,1)S(1)}, bf16[64,1280]{1,0:T(8,128)(2,1)S(1)}, u32[]{:S(2)}, u32[]{:S(2)}) collective-permute-start(bf16[64,1280]{1,0:T(8,128)(2,1)S(1)} %get-tuple-element.15.refs_0_), channel_id=1, source_target_pairs={{0,64},{1,65},{2,66},{3,67},{4,68},{5,69},{6,70},{7,71},{8,72},{9,... | collective-permute-start | bytes 491528 | tf_op jit(solution)/shard_map/ppermute | solution.py:43
  48.5 9.9 %collective-permute-start.8 = (bf16[64,1280]{1,0:T(8,128)(2,1)S(1)}, bf16[64,1280]{1,0:T(8,128)(2,1)S(1)}, u32[]{:S(2)}, u32[]{:S(2)}) collective-permute-start(bf16[64,1280]{1,0:T(8,128)(2,1)S(1)} %get-tuple-element.15.refs_0_), channel_id=1, source_target_pairs={{0,192},{1,193},{2,194},{3,195},{4,196},{5,197},{6,198},{7,199},{8... | collective-permute-start | bytes 491528 | tf_op jit(solution)/shard_map/ppermute | solution.py:43
  51.5 16.7 %copy-start.7 = (bf16[64,1280]{1,0:T(8,128)(2,1)}, bf16[64,1280]{1,0:T(8,128)(2,1)S(1)}, u32[]{:S(2)}) copy-start(bf16[64,1280]{1,0:T(8,128)(2,1)S(1)} %collective-permute-done.6.refs_1_) | copy-start | bytes 491524
  57.3 10.9 %copy-start.8 = (bf16[64,1280]{1,0:T(8,128)(2,1)}, bf16[64,1280]{1,0:T(8,128)(2,1)S(1)}, u32[]{:S(2)}) copy-start(bf16[64,1280]{1,0:T(8,128)(2,1)S(1)} %collective-permute-done.7.refs_2_) | copy-start | bytes 491524
  58.5 9.7 %copy-start.9 = (bf16[64,1280]{1,0:T(8,128)(2,1)}, bf16[64,1280]{1,0:T(8,128)(2,1)S(1)}, u32[]{:S(2)}) copy-start(bf16[64,1280]{1,0:T(8,128)(2,1)S(1)} %collective-permute-done.8.refs_3_) | copy-start | bytes 491524
  58.5 9.6 %collective-permute-start.9 = (bf16[64,1280]{1,0:T(8,128)(2,1)S(1)}, bf16[64,1280]{1,0:T(8,128)(2,1)S(1)}, u32[]{:S(2)}, u32[]{:S(2)}) collective-permute-start(bf16[64,1280]{1,0:T(8,128)(2,1)S(1)} %get-tuple-element.15.refs_0_), channel_id=1, source_target_pairs={{0,144},{1,145},{2,146},{3,147},{4,148},{5,149},{6,150},{7,151},{8... | collective-permute-start | bytes 491528 | tf_op jit(solution)/shard_map/ppermute | solution.py:43
  58.5 9.6 %collective-permute-start.10 = (bf16[64,1280]{1,0:T(8,128)(2,1)S(1)}, bf16[64,1280]{1,0:T(8,128)(2,1)S(1)}, u32[]{:S(2)}, u32[]{:S(2)}) collective-permute-start(bf16[64,1280]{1,0:T(8,128)(2,1)S(1)} %get-tuple-element.15.refs_0_), channel_id=1, source_target_pairs={{0,80},{1,81},{2,82},{3,83},{4,84},{5,85},{6,86},{7,87},{8,88},{9,... | collective-permute-start | bytes 491528 | tf_op jit(solution)/shard_map/ppermute | solution.py:43
  62.0 6.1 %collective-permute-start.11 = (bf16[64,1280]{1,0:T(8,128)(2,1)S(1)}, bf16[64,1280]{1,0:T(8,128)(2,1)S(1)}, u32[]{:S(2)}, u32[]{:S(2)}) collective-permute-start(bf16[64,1280]{1,0:T(8,128)(2,1)S(1)} %get-tuple-element.15.refs_0_), channel_id=1, source_target_pairs={{0,208},{1,209},{2,210},{3,211},{4,212},{5,213},{6,214},{7,215},{8... | collective-permute-start | bytes 491528 | tf_op jit(solution)/shard_map/ppermute | solution.py:43
  62.1 6.1 %collective-permute-start.12 = (bf16[64,1280]{1,0:T(8,128)(2,1)S(1)}, bf16[64,1280]{1,0:T(8,128)(2,1)S(1)}, u32[]{:S(2)}, u32[]{:S(2)}) collective-permute-start(bf16[64,1280]{1,0:T(8,128)(2,1)S(1)} %get-tuple-element.15.refs_0_), channel_id=1, source_target_pairs={{0,16},{1,17},{2,18},{3,19},{4,20},{5,21},{6,22},{7,23},{8,24},{9,... | collective-permute-start | bytes 491528 | tf_op jit(solution)/shard_map/ppermute | solution.py:43
  68.1 0.7 copy-start.10
  68.1 0.7 copy-start.11
  68.1 0.8 copy-start.12
  68.9 0.6 copy-start.13
  80.4 58.8 %collective-permute-start.14 = (bf16[512,4096]{1,0:T(8,128)(2,1)}, bf16[512,4096]{1,0:T(8,128)(2,1)}, u32[]{:S(2)}, u32[]{:S(2)}) collective-permute-start(bf16[512,4096]{1,0:T(8,128)(2,1)} %normalize.1.own_low.own_high), channel_id=1, source_target_pairs={{0,32},{1,33},{2,34},{3,35},{4,36},{5,37},{6,38},{7,39},{8,40},{9,... | collective-permute-start | bytes 12582920 | tf_op jit(solution)/shard_map/ppermute | solution.py:43
  81.2 7.0 %collective-permute-start.13 = (f32[64,1280]{1,0:T(8,128)S(1)}, f32[64,1280]{1,0:T(8,128)S(1)}, u32[]{:S(2)}, u32[]{:S(2)}) collective-permute-start(f32[64,1280]{1,0:T(8,128)S(1)} %pad_maximum_fusion.4), channel_id=1, source_target_pairs={{0,32},{1,33},{2,34},{3,35},{4,36},{5,37},{6,38},{7,39},{8,40},{9,... | collective-permute-start | bytes 983048 | tf_op jit(solution)/shard_map/ppermute | solution.py:43
  171.6 3.4 %collective-permute-start.15 = (bf16[512,1024]{1,0:T(8,128)(2,1)}, bf16[512,1024]{1,0:T(8,128)(2,1)S(1)}, u32[]{:S(2)}, u32[]{:S(2)}) collective-permute-start(bf16[512,1024]{1,0:T(8,128)(2,1)} %get-tuple-element.21), channel_id=1, source_target_pairs={{0,32},{1,33},{2,34},{3,35},{4,36},{5,37},{6,38},{7,39},{8,40},{9,... | collective-permute-start | bytes 3145736 | tf_op jit(solution)/shard_map/ppermute | solution.py:43
  175.0 1.0 copy-start.1
Sparse Core Ops, SparseCore 0:
  72.9 66.2 all-gather.1

commit v2 on v1

--- a/solution.py
+++ b/solution.py
@@ -1,5 +1,3 @@
-import functools
-
 import jax
 import jax.numpy as jnp
 from jax import lax
@@ -117,119 +115,97 @@
     )(at, *blocks)
 
 
-def norm_kernel(high_ref, own, other, gain, out):
+def norm_kernel(where_ref, own, other, gain, mine, theirs):
     first, second = own[...].astype(jnp.float32), other[...].astype(jnp.float32)
     square = jnp.sum(first * first + second * second, axis=-1, keepdims=True)
     scale = lax.rsqrt(square * (1.0 / D) + 1e-05)
-    keep = high_ref[0] == 0
-    for a, b, start in ((first, second, 0), (second, first, HALF)):
-        values = jnp.where(keep, a, b) * scale * gain[:, start : start + HALF]
-        out[:, start : start + HALF] = values.astype(jnp.bfloat16)
-
-
-def normalize(high, own, other, gain):
+    keep = where_ref[1] == 0
+    halves = [
+        (jnp.where(keep, a, b) * scale * gain[:, start : start + HALF]).astype(jnp.bfloat16)
+        for a, b, start in ((first, second, 0), (second, first, HALF))
+    ]
+
+    def fill(by_z, by_plane):
+        for z in range(NZ):
+            for y in range(NY):
+                start = z * 512 + y * 256
+                by_z[:, start : start + 256] = halves[y][:, z * 256 : (z + 1) * 256]
+        for y in range(NY):
+            for x in range(NX):
+                start = (y * NX + x) * 512
+                starts = [z * 256 + x * 64 for z in range(NZ)]
+                by_plane[:, start : start + 512] = jnp.concatenate(
+                    [halves[y][:, at : at + 64] for at in starts], axis=1
+                )
+
+    @pl.when(where_ref[0] == 0)
+    def _():
+        fill(mine, theirs)
+
+    @pl.when(where_ref[0] == 1)
+    def _():
+        fill(theirs, mine)
+
+
+def normalize(where, own, other, gain):
     tile = 64
-    count = own.shape[0]
+    shape = jax.ShapeDtypeStruct((SEQ, D), jnp.bfloat16)
     rows = pl.BlockSpec((tile, HALF), lambda i, w: (i, 0))
+    out = pl.BlockSpec((tile, D), lambda i, w: (i, 0))
     return pl.pallas_call(
         norm_kernel,
-        out_shape=jax.ShapeDtypeStruct((count, D), jnp.bfloat16),
+        out_shape=(shape, shape),
         grid_spec=pltpu.PrefetchScalarGridSpec(
             num_scalar_prefetch=1,
-            grid=(count // tile,),
+            grid=(SEQ // tile,),
             in_specs=[rows, rows, pl.BlockSpec((1, D), lambda i, w: (0, 0))],
-            out_specs=pl.BlockSpec((tile, D), lambda i, w: (i, 0)),
+            out_specs=(out, out),
         ),
         compiler_params=pltpu.CompilerParams(vmem_limit_bytes=VMEM_LIMIT),
         cost_estimate=pl.CostEstimate(
-            flops=8 * count * D, transcendentals=0, bytes_accessed=4 * count * D
+            flops=8 * SEQ * D, transcendentals=0, bytes_accessed=6 * SEQ * D
         ),
         name="normalize",
-    )(high, own, other, gain.reshape(1, D))
-
-
-def project_kernel(
-    core_ref, own_low, own_high, sib_low, sib_high, by_z, by_plane, out, rows
-):
-    for i, (low, high) in enumerate(((own_low, own_high), (sib_low, sib_high))):
-        rows[i * SEQ : (i + 1) * SEQ, :512] = low[...]
-        rows[i * SEQ : (i + 1) * SEQ, 512:] = high[...]
-
-    def add(weights):
-        part = jnp.dot(rows[...], weights, preferred_element_type=jnp.float32)
-        part = part.reshape(out.shape)
-
-        @pl.when(pl.program_id(0) == 0)
-        def _():
-            out[...] = part
-
-        @pl.when(pl.program_id(0) > 0)
-        def _():
-            out[...] += part
-
-    @pl.when(core_ref[0] == 0)
-    def _():
-        add(jnp.concatenate([by_z[i * 256 : (i + 1) * 256] for i in (0, 2, 1, 3)]))
-
-    @pl.when(core_ref[0] == 1)
-    def _():
-        add(
-            jnp.concatenate(
-                [
-                    by_plane[y, :, z].reshape(256, by_plane.shape[-1])
-                    for y in range(NY)
-                    for z in range(2)
-                ]
-            )
-        )
-
-
-def project(core, normed, weights):
-    width = weights.shape[1]
-    steps = NZ // 2
-    low = pl.BlockSpec((SEQ, 512), lambda t, core: (0, t))
-    high = pl.BlockSpec((SEQ, 512), lambda t, core: (0, steps + t))
-    shape = (2, SEQ, width)
-    own, sib = normed
+    )(where, own, other, gain.reshape(1, D))
+
+
+def project_kernel(rows, weights, out):
+    out[...] = jnp.dot(rows[...], weights[...], preferred_element_type=jnp.float32)
+
+
+def project(rows, weights):
+    count, width = rows.shape[0], weights.shape[1]
+    tile = 2 * HD
     return pl.pallas_call(
         project_kernel,
-        out_shape=jax.ShapeDtypeStruct(shape, jnp.float32),
-        grid_spec=pltpu.PrefetchScalarGridSpec(
-            num_scalar_prefetch=1,
-            grid=(steps,),
-            in_specs=[low, high, low, high]
-            + [
-                pl.BlockSpec((1024, width), lambda t, core: (jnp.where(core[0] == 0, t, 0), 0)),
-                pl.BlockSpec(
-                    (NY, NX, 2, 64, width),
-                    lambda t, core: (0, 0, jnp.where(core[0] == 0, 0, t), 0, 0),
-                ),
-            ],
-            out_specs=pl.BlockSpec(shape, lambda t, core: (0, 0, 0)),
-            scratch_shapes=[pltpu.VMEM((2 * SEQ, 1024), jnp.bfloat16)],
-        ),
-        compiler_params=pltpu.CompilerParams(vmem_limit_bytes=VMEM_LIMIT),
+        out_shape=jax.ShapeDtypeStruct((count, width), jnp.float32),
+        grid=(width // tile,),
+        in_specs=[
+            pl.BlockSpec((count, D), lambda n: (0, 0), pipeline_mode=pl.Buffered(1)),
+            pl.BlockSpec((D, tile), lambda n: (0, n)),
+        ],
+        out_specs=pl.BlockSpec((count, tile), lambda n: (0, n)),
+        compiler_params=pltpu.CompilerParams(vmem_limit_bytes=32 << 20),
         cost_estimate=pl.CostEstimate(
-            flops=4 * SEQ * D * width,
+            flops=2 * count * D * width,
             transcendentals=0,
-            bytes_accessed=2 * D * width + 4 * SEQ * D + 8 * SEQ * width,
+            bytes_accessed=2 * D * width + 2 * count * D + 4 * count * width,
         ),
         name="project",
-    )(core, own, own, sib, sib, weights, weights.reshape(NY, NX, NZ, 64, width))
+    )(rows, weights)
 
 
 def turn(values, cosine, sine):
     return values * cosine + pltpu.roll(values, HD // 2, 1) * sine
 
 
-def attend_kernel(at_ref, q_ref, kv_ref, cos_ref, sin_ref, mine, theirs, key, value):
-    row = pl.program_id(0)
-    length = at_ref[row]
+def attend_kernel(at_ref, q_ref, kv_ref, cos_ref, sin_ref, out, key, value):
+    length = at_ref[0]
     cosine, sine = cos_ref[...], sin_ref[...]
     unit = D**-0.5
     tile = 256
 
-    @pl.when(pl.program_id(1) == 0)
+    @pl.when(pl.program_id(0) == 0)
     def _():
         key[...] = turn(kv_ref[0, :, :HD] * unit, cosine, sine).astype(jnp.bfloat16)
         value[...] = (kv_ref[0, :, HD:] * unit).astype(jnp.bfloat16)
@@ -241,7 +217,6 @@
         turn(q_ref[0, :, h * HD : (h + 1) * HD] * unit, cosine, sine).astype(jnp.bfloat16)
         for h in heads
     ]
-    results = {}
     for block in range(SEQ // tile):
         start, reach = block * tile, (block + 1) * tile
         allowed = [jnp.where((t <= s) & (t + start < length), 0.0, -1e30)]
@@ -264,53 +239,38 @@
         )
         mixed = mixed * scale
         for h in heads:
-            results[start, h * HD] = jnp.where(
+            out[start:reach, h * HD : (h + 1) * HD] = jnp.where(
                 live, mixed[h * tile : (h + 1) * tile], 0.0
             ).astype(jnp.bfloat16)
 
-    def fill(out):
-        for (start, column), part in results.items():
-            out[start : start + tile, column : column + HD] = part
-
-    pl.when(row == 0)(lambda: fill(mine))
-    pl.when(row == 1)(lambda: fill(theirs))
-
-
-def attend(lens, column, proj, cosine, sine):
+
+def attend(length, row, proj, cosine, sine, columns, column):
     width = QPK * HD
     count = width // (2 * HD)
-    at = jnp.concatenate([lens, jnp.reshape(column // (2 * HD), (1,))])
+    at = jnp.stack([length, jnp.asarray(column // (2 * HD), jnp.int32)])
     return pl.pallas_call(
         attend_kernel,
-        out_shape=(
-            jax.ShapeDtypeStruct((SEQ, 2 * width), jnp.bfloat16),
-            jax.ShapeDtypeStruct((SEQ, width), jnp.bfloat16),
-        ),
+        out_shape=jax.ShapeDtypeStruct((SEQ, columns), jnp.bfloat16),
         grid_spec=pltpu.PrefetchScalarGridSpec(
             num_scalar_prefetch=1,
-            grid=(2, count),
+            grid=(count,),
             in_specs=[
-                pl.BlockSpec((1, SEQ, 2 * HD), lambda r, j, at: (r, 0, j)),
-                pl.BlockSpec((1, SEQ, 2 * HD), lambda r, j, at: (r, 0, count)),
-                pl.BlockSpec((SEQ, HD), lambda r, j, at: (0, 0)),
-                pl.BlockSpec((SEQ, HD), lambda r, j, at: (0, 0)),
+                pl.BlockSpec((1, SEQ, 2 * HD), lambda j, at: (row, 0, j)),
+                pl.BlockSpec((1, SEQ, 2 * HD), lambda j, at: (row, 0, count)),
+                pl.BlockSpec((SEQ, HD), lambda j, at: (0, 0)),
+                pl.BlockSpec((SEQ, HD), lambda j, at: (0, 0)),
             ],
-            out_specs=(
-                pl.BlockSpec(
-                    (SEQ, 2 * HD), lambda r, j, at: (0, at[2] + jnp.where(r == 0, j, count - 1))
-                ),
-                pl.BlockSpec((SEQ, 2 * HD), lambda r, j, at: (0, jnp.where(r == 0, 0, j))),
-            ),
+            out_specs=pl.BlockSpec((SEQ, 2 * HD), lambda j, at: (0, at[1] + j)),
             scratch_shapes=[
                 pltpu.VMEM((SEQ, HD), jnp.bfloat16),
                 pltpu.VMEM((SEQ, HD), jnp.bfloat16),
             ],
         ),
-        compiler_params=pltpu.CompilerParams(vmem_limit_bytes=VMEM_LIMIT),
+        compiler_params=pltpu.CompilerParams(vmem_limit_bytes=24 << 20),
         cost_estimate=pl.CostEstimate(
-            flops=8 * SEQ * SEQ * width,
-            transcendentals=2 * SEQ * SEQ * width // HD,
-            bytes_accessed=12 * SEQ * width,
+            flops=4 * SEQ * SEQ * width,
+            transcendentals=SEQ * SEQ * width // HD,
+            bytes_accessed=6 * SEQ * width,
         ),
         name="attend",
     )(at, proj, proj, cosine, sine)
@@ -321,7 +281,7 @@
 
 
 def insert(column, part, context):
-    width = 2 * HD
+    width = 4 * HD
     return pl.pallas_call(
         insert_kernel,
         out_shape=jax.ShapeDtypeStruct(context.shape, context.dtype),
@@ -384,7 +344,6 @@
         ),
         sibling,
     )
-    lens = jnp.stack([lengths[0], states[64, 0].astype(jnp.int32)])
 
     places_at = [jnp.where(core == 0, y * NX + x, z)]
     for (dx, dy), dz in zip(NEAR, NEAR_Z):
@@ -432,16 +391,17 @@
         for i, v in enumerate(both)
     ]
 
-    core_id = jnp.reshape(core, (1,)).astype(jnp.int32)
-    high_id = jnp.reshape(lax.axis_index("tensor"), (1,)).astype(jnp.int32)
     full = lax.all_gather(whole, AXES, axis=0, tiled=True, axis_index_groups=far_groups())
-    kept = normalize(high_id, own_tokens, after(other_tokens, whole), norm_gain)
-    normed = (kept, send(kept, sibling))
-
-    full, *outs = lax.optimization_barrier((full, *outs))
-    proj = project(core_id, normed, full)
-    context, given = attend(lens, core * QPK * HD, proj, cosine, sine)
-    context = insert((1 - core) * QPK * HD, send(given, sibling), context)
+    where = jnp.stack([core, lax.axis_index("tensor")]).astype(jnp.int32)
+    kept, given = normalize(where, own_tokens, after(other_tokens, whole), norm_gain)
+    normed = jnp.concatenate([kept, send(given, sibling)])
+    full = after(full, normed[-16:, -HD:], *outs)
+    proj = project(normed, full).reshape(2, SEQ, GROUP)
+    width = QPK * HD
+    given = attend(states[64, 0].astype(jnp.int32), 1, proj, cosine, sine, width, 0)
+    got = send(given, sibling)
+    context = attend(lengths[0], 0, proj, cosine, sine, 2 * width, core * width)
+    context = insert((1 - core) * width, got, context)
     return outs[0], outs[1], context[None]
 
 

time: 187 us -> 182 us (0.973)
  waiting for transfers between devices: 80.6 us -> 68.3 us
  other arithmetic: 9.73 us -> 18 us
  Pallas kernels: 46.6 us -> 40.3 us
  local copies, waits for them, and re-layouts: 5.55 us -> 11.1 us
    all_gather x1, waiting for transfers between devices: 49.3 us -> 36.5 us  [per_device(): lax.all_gather(whole, AXES, axis=0, tiled=True, axis_index_groups=far_gro...]
    concatenate x1, other arithmetic: 0.66 us -> 8.06 us  [per_device(): normed = jnp.concatenate([kept, send(given, sibling)])]
    unnamed x28 -> x32, local copies, waits for them, and re-layouts: 2.39 us -> 7.94 us
    pallas_call x3 -> x4, Pallas kernels: 40.1 us -> 35 us  [the longest x1 13.6 us: project(): pl.pallas_call(project_kernel, out_shape=jax.ShapeDtypeStruct((count, wid...]
  transfers between devices with their start and end apart: 17 -> 17, of which waited for: 10 -> 11; matrix products, arithmetic and copies ran while one was open for 6% -> 10% of each run, Pallas kernels for 4% -> 9%
where the time goes in v2:
time: 182 us; the launch traced here: 181 us
  waiting for transfers between devices  68.3 us (38%)
  Pallas kernels  40.3 us (22%)
  starting transfers between devices  27.2 us (15%)
  other arithmetic  18 us (10%)
  between operations  16.2 us (9%)
  local copies, waits for them, and re-layouts  11.1 us (6%)
    all_gather x1, waiting for transfers between devices, per_device(): lax.all_gather(whole, AXES, axis=0, tiled=True, axis_index_groups=far_gro...  36.5 us
    ppermute x16, waiting for transfers between devices, send(): return lax.ppermute(value, AXES, pairs(target))  31.7 us
    ppermute x16, starting transfers between devices, send(): return lax.ppermute(value, AXES, pairs(target))  27.2 us
    pallas_call x1, Pallas kernels, project(): pl.pallas_call(project_kernel, out_shape=jax.ShapeDtypeStruct((count, wid...  13.6 us
    pallas_call x2, Pallas kernels, attend(): pl.pallas_call(attend_kernel, out_shape=jax.ShapeDtypeStruct((SEQ, column...  11.6 us
    pallas_call x1, Pallas kernels, normalize(): pl.pallas_call(norm_kernel, out_shape=(shape, shape), grid_spec=pltpu.Pre...  9.9 us
    concatenate x1, other arithmetic, per_device(): normed = jnp.concatenate([kept, send(given, sibling)])  8.06 us
    unnamed x32, local copies, waits for them, and re-layouts  7.94 us
  transfers between devices with their start and end apart: 17, of which 11 were waited for; matrix products, arithmetic and copies ran while one was open for 10% of the time, Pallas kernels for 9%

profile of v2, /device:TPU:1, one launch (start us, length us, event | category | flops | bytes accessed | tf_op | source)
XLA Modules:
  0.0 181.1 jit_solution(14542226792369705728)
XLA Ops:
  7.9 1.5 multiply_bitcast_fusion
  9.4 1.2 concatenate.43
  10.5 3.2 %collective-permute-start = (f32[264,1280]{1,0:T(8,128)}, f32[264,1280]{1,0:T(8,128)}, u32[]{:S(2)}, u32[]{:S(2)}) collective-permute-start(f32[264,1280]{1,0:T(8,128)} %concatenate.43), channel_id=1, source_target_pairs={{0,32},{1,33},{2,34},{3,35},{4,36},{5,37},{6,38},{7,39},{8,40},{9,... | collective-permute-start | bytes 4055048 | tf_op jit(solution)/shard_map/ppermute | solution.py:41
  13.8 1.2 collective-permute-start.5
  15.8 1.1 collective-permute-done
  16.8 1.5 slice_add_fusion
  19.4 1.8 collective-permute-start.4
  22.7 1.1 collective-permute-start.1
  23.9 7.1 %collective-permute-done.4 = f32[72,1280]{1,0:T(8,128)S(1)} collective-permute-done((f32[72,1280]{1,0:T(8,128)S(1)}, f32[72,1280]{1,0:T(8,128)S(1)}, u32[]{:S(2)}, u32[]{:S(2)}) %collective-permute-start.4) | collective-permute-done | bytes 368672 | tf_op jit(solution)/shard_map/ppermute | solution.py:41
  31.0 7.0 %collective-permute-done.3 = f32[72,1280]{1,0:T(8,128)S(1)} collective-permute-done((f32[72,1280]{1,0:T(8,128)S(1)}, f32[72,1280]{1,0:T(8,128)S(1)}, u32[]{:S(2)}, u32[]{:S(2)}) %collective-permute-start.3) | collective-permute-done | bytes 368672 | tf_op jit(solution)/shard_map/ppermute | solution.py:41
  38.0 1.5 collective-permute-done.2
  40.1 1.1 slice_select_fusion.9
  42.0 5.9 %collective-permute-start.6 = (bf16[64,1280]{1,0:T(8,128)(2,1)S(1)}, bf16[64,1280]{1,0:T(8,128)(2,1)S(1)}, u32[]{:S(2)}, u32[]{:S(2)}) collective-permute-start(bf16[64,1280]{1,0:T(8,128)(2,1)S(1)} %get-tuple-element.13.refs_0_), channel_id=1, source_target_pairs={{0,128},{1,129},{2,130},{3,131},{4,132},{5,133},{6,134},{7,135},{8... | collective-permute-start | bytes 491528 | tf_op jit(solution)/shard_map/ppermute | solution.py:41
  47.9 1.6 collective-permute-start.7
  49.6 2.8 %collective-permute-start.8 = (bf16[64,1280]{1,0:T(8,128)(2,1)S(1)}, bf16[64,1280]{1,0:T(8,128)(2,1)S(1)}, u32[]{:S(2)}, u32[]{:S(2)}) collective-permute-start(bf16[64,1280]{1,0:T(8,128)(2,1)S(1)} %get-tuple-element.13.refs_0_), channel_id=1, source_target_pairs={{0,192},{1,193},{2,194},{3,195},{4,196},{5,197},{6,198},{7,199},{8... | collective-permute-start | bytes 491528 | tf_op jit(solution)/shard_map/ppermute | solution.py:41
  52.5 5.8 %collective-permute-done.7.refs_2_ = bf16[64,1280]{1,0:T(8,128)(2,1)S(1)} collective-permute-done((bf16[64,1280]{1,0:T(8,128)(2,1)S(1)}, bf16[64,1280]{1,0:T(8,128)(2,1)S(1)}, u32[]{:S(2)}, u32[]{:S(2)}) %collective-permute-start.7) | collective-permute-done | bytes 163872 | tf_op jit(solution)/shard_map/ppermute | solution.py:41
  58.3 1.2 collective-permute-done.8.refs_3_
  59.7 3.4 %collective-permute-start.10 = (bf16[64,1280]{1,0:T(8,128)(2,1)S(1)}, bf16[64,1280]{1,0:T(8,128)(2,1)S(1)}, u32[]{:S(2)}, u32[]{:S(2)}) collective-permute-start(bf16[64,1280]{1,0:T(8,128)(2,1)S(1)} %get-tuple-element.13.refs_0_), channel_id=1, source_target_pairs={{0,80},{1,81},{2,82},{3,83},{4,84},{5,85},{6,86},{7,87},{8,88},{9,... | collective-permute-start | bytes 491528 | tf_op jit(solution)/shard_map/ppermute | solution.py:41
  63.1 2.7 %collective-permute-start.12 = (bf16[64,1280]{1,0:T(8,128)(2,1)S(1)}, bf16[64,1280]{1,0:T(8,128)(2,1)S(1)}, u32[]{:S(2)}, u32[]{:S(2)}) collective-permute-start(bf16[64,1280]{1,0:T(8,128)(2,1)S(1)} %get-tuple-element.13.refs_0_), channel_id=1, source_target_pairs={{0,16},{1,17},{2,18},{3,19},{4,20},{5,21},{6,22},{7,23},{8,24},{9,... | collective-permute-start | bytes 491528 | tf_op jit(solution)/shard_map/ppermute | solution.py:41
  66.3 1.8 %collective-permute-done.5.other = bf16[512,2048]{1,0:T(8,128)(2,1)} collective-permute-done((bf16[512,2048]{1,0:T(8,128)(2,1)}, bf16[512,2048]{1,0:T(8,128)(2,1)}, u32[]{:S(2)}, u32[]{:S(2)}) %collective-permute-start.5) | collective-permute-done | bytes 2097184 | tf_op jit(solution)/shard_map/ppermute | solution.py:41
  69.8 3.2 %place.1 = bf16[512,1280]{1,0:T(8,128)(2,1)} custom-call(s32[8]{0:T(128)} %broadcast_multiply_fusion.at_ref, bf16[64,1280]{1,0:T(8,128)(2,1)} %copy-done.5, bf16[64,1280]{1,0:T(8,128)(2,1)} %copy-done.9, bf16[64,1280]{1,0:T(8,128)(2,1)} %copy-done.10, bf16[64,1280]{1,0:T(8,128)(2,1)} %copy-done.11, bf16[64,1280]{1,0:T(8,128)(2,1)} %copy-done.12, ...), custom_call_target="tpu_custom_call" | custom-call | bytes 2621440 | tf_op jit(solution)/shard_map/place/pallas_call | solution.py:101
  73.1 1.2 slice.72
  75.5 9.9 %normalize.1 = (bf16[512,4096]{1,0:T(8,128)(2,1)}, bf16[512,4096]{1,0:T(8,128)(2,1)}) custom-call(s32[2]{0:T(128)} %get-tuple-element.45.where_ref, bf16[512,2048]{1,0:T(8,128)(2,1)} %bitcast.18.own, bf16[512,2048]{1,0:T(8,128)(2,1)} %collective-permute-done.5.other, f32[1,4096]{1,0:T(1,128)} %bitcast.39), custom_call_target="tpu_custom_call" | custom-call | flops 16777216 | bytes 12582912 | tf_op jit(solution)/shard_map/normalize/pallas_call | solution.py:155
  87.5 5.6 %collective-permute-done.13 = f32[64,1280]{1,0:T(8,128)S(1)} collective-permute-done((f32[64,1280]{1,0:T(8,128)S(1)}, f32[64,1280]{1,0:T(8,128)S(1)}, u32[]{:S(2)}, u32[]{:S(2)}) %collective-permute-start.13) | collective-permute-done | bytes 327712 | tf_op jit(solution)/shard_map/ppermute | solution.py:41
  94.6 8.1 %pad_maximum_fusion.rows = bf16[1024,4096]{1,0:T(8,128)(2,1)} fusion(bf16[512,4096]{1,0:T(8,128)(2,1)} %collective-permute-done.14, bf16[512,4096]{1,0:T(8,128)(2,1)} %get-tuple-element.16), kind=kLoop, calls=%fused_computation | loop fusion | flops 16777216 | bytes 16777216 | tf_op jit(solution)/shard_map/concatenate | solution.py:397
  102.7 36.5 %all-gather.2.cloned.1.call-done.weights = bf16[4096,1280]{1,0:T(8,128)(2,1)} async-done(((bf16[512,1280]{1,0:T(8,128)(2,1)}), bf16[4096,1280]{1,0:T(8,128)(2,1)}) %all-gather.2.cloned.1.call-update) | async-done | bytes 10485776 | tf_op jit(solution)/shard_map/all_gather | solution.py:394
  139.2 3.4 %copy-done.2 = bf16[1024,4096]{1,0:T(8,128)(2,1)S(1)} copy-done((bf16[1024,4096]{1,0:T(8,128)(2,1)S(1)}, bf16[1024,4096]{1,0:T(8,128)(2,1)}, u32[]{:S(2)}) %copy-start.2) | copy-done | bytes 8388632
  142.6 13.6 %project.1 = f32[1024,1280]{1,0:T(8,128)S(1)} custom-call(bf16[1024,4096]{1,0:T(8,128)(2,1)S(1)} %copy-done.2, bf16[4096,1280]{1,0:T(8,128)(2,1)} %all-gather.2.cloned.1.call-done.weights), custom_call_target="tpu_custom_call" | custom-call | flops 10737418240 | bytes 24117248 | tf_op jit(solution)/shard_map/project/pallas_call | solution.py:179
  156.1 5.5 %attend.2 = bf16[512,1024]{1,0:T(8,128)(2,1)S(1)} custom-call(s32[2]{0:T(128)S(1)} %get-tuple-element.44.at_ref, f32[2,512,1280]{2,1,0:T(8,128)S(1)} %bitcast.33, f32[2,512,1280]{2,1,0:T(8,128)S(1)} %bitcast.34, f32[512,128]{1,0:T(8,128)S(1)} %get-tuple-element.48.cos_ref, f32[512,128]{1,0:T(8,128)S(1)} %get-tuple-element.49.sin_ref), custom_call_target="tpu_custom_call" | custom-call | flops 1073741824 | bytes 3145728 | tf_op jit(solution)/shard_map/attend/pallas_call | solution.py:251
  162.6 2.5 %copy-done.1 = f32[1024,1280]{1,0:T(8,128)S(1)} copy-done((f32[1024,1280]{1,0:T(8,128)S(1)}, f32[1024,1280]{1,0:T(8,128)}, u32[]{:S(2)}) %copy-start.1) | copy-done | bytes 5242904
  165.1 6.1 %attend.3._ = bf16[512,2048]{1,0:T(8,128)(2,1)} custom-call(s32[2]{0:T(128)S(1)} %pad_add_fusion.2.at_ref, f32[2,512,1280]{2,1,0:T(8,128)S(1)} %bitcast.35, f32[2,512,1280]{2,1,0:T(8,128)S(1)} %bitcast.36, f32[512,128]{1,0:T(8,128)S(1)} %get-tuple-element.48.cos_ref, f32[512,128]{1,0:T(8,128)S(1)} %get-tuple-element.49.sin_ref), custom_call_target="tpu_custom_call" | custom-call | flops 1073741824 | bytes 3145728 | tf_op jit(solution)/shard_map/attend/pallas_call | solution.py:251
  172.2 2.0 %insert.1 = bf16[512,2048]{1,0:T(8,128)(2,1)} custom-call(s32[1]{0:T(128)} %bitcast.19.at_ref, bf16[512,1024]{1,0:T(8,128)(2,1)} %copy-done.4, bf16[512,2048]{1,0:T(8,128)(2,1)} %attend.3._), custom_call_target="tpu_custom_call", output_to_operand_aliasing={{}: (2, {})} | custom-call | bytes 2097152 | tf_op jit(solution)/shard_map/insert/pallas_call | solution.py:285
  (70 shorter events, 12.8 us)
Async XLA Ops:
  7.2 132.0 %all-gather.2.cloned.1.call-start = ((), (), s32[]{:S(2)}) async-start(), calls=%async_computation | async-start | bytes 11796480 | tf_op jit(solution)/shard_map/all_gather | solution.py:394
  7.9 7.8 %copy-start.6 = (f32[32,2560]{1,0:T(8,128)S(1)}, f32[32,2560]{1,0:T(8,128)}, u32[]{:S(2)}) copy-start(f32[32,2560]{1,0:T(8,128)} %param.10) | copy-start | bytes 983044
  9.3 6.4 %copy-start.7 = (f32[32,2560]{1,0:T(8,128)S(1)}, f32[32,2560]{1,0:T(8,128)}, u32[]{:S(2)}) copy-start(f32[32,2560]{1,0:T(8,128)} %param.9) | copy-start | bytes 983044
  9.4 7.5 %copy-start.3 = (f32[1,256,2560]{2,1,0:T(8,128)S(1)}, f32[1,256,2560]{2,1,0:T(8,128)}, u32[]{:S(2)}) copy-start(f32[1,256,2560]{2,1,0:T(8,128)} %param.7) | copy-start | bytes 7864324
  10.5 6.3 %collective-permute-start = (f32[264,1280]{1,0:T(8,128)}, f32[264,1280]{1,0:T(8,128)}, u32[]{:S(2)}, u32[]{:S(2)}) collective-permute-start(f32[264,1280]{1,0:T(8,128)} %concatenate.43), channel_id=1, source_target_pairs={{0,32},{1,33},{2,34},{3,35},{4,36},{5,37},{6,38},{7,39},{8,40},{9,... | collective-permute-start | bytes 4055048 | tf_op jit(solution)/shard_map/ppermute | solution.py:41
  13.8 54.3 %collective-permute-start.5 = (bf16[512,2048]{1,0:T(8,128)(2,1)}, bf16[512,2048]{1,0:T(8,128)(2,1)}, u32[]{:S(2)}, u32[]{:S(2)}) collective-permute-start(bf16[512,2048]{1,0:T(8,128)(2,1)} %bitcast.18.own), channel_id=1, source_target_pairs={{0,1},{1,0},{2,3},{3,2},{4,5},{5,4},{6,7},{7,6},{8,9},{9,8},{10,11... | collective-permute-start | bytes 6291464 | tf_op jit(solution)/shard_map/ppermute | solution.py:41
  19.4 11.6 %collective-permute-start.4 = (f32[72,1280]{1,0:T(8,128)S(1)}, f32[72,1280]{1,0:T(8,128)S(1)}, u32[]{:S(2)}, u32[]{:S(2)}) collective-permute-start(f32[72,1280]{1,0:T(8,128)S(1)} %get-tuple-element.40), channel_id=1, source_target_pairs={{0,128},{1,129},{2,130},{3,131},{4,132},{5,133},{6,134},{7,135},{8... | collective-permute-start | bytes 1105928 | tf_op jit(solution)/shard_map/ppermute | solution.py:41
  21.1 16.9 %collective-permute-start.3 = (f32[72,1280]{1,0:T(8,128)S(1)}, f32[72,1280]{1,0:T(8,128)S(1)}, u32[]{:S(2)}, u32[]{:S(2)}) collective-permute-start(f32[72,1280]{1,0:T(8,128)S(1)} %get-tuple-element.39), channel_id=1, source_target_pairs={{0,192},{1,193},{2,194},{3,195},{4,196},{5,197},{6,198},{7,199},{8... | collective-permute-start | bytes 1105928 | tf_op jit(solution)/shard_map/ppermute | solution.py:41
  22.0 17.5 %collective-permute-start.2 = (f32[72,1280]{1,0:T(8,128)S(1)}, f32[72,1280]{1,0:T(8,128)S(1)}, u32[]{:S(2)}, u32[]{:S(2)}) collective-permute-start(f32[72,1280]{1,0:T(8,128)S(1)} %get-tuple-element.38), channel_id=1, source_target_pairs={{0,64},{1,65},{2,66},{3,67},{4,68},{5,69},{6,70},{7,71},{8,72},{9,... | collective-permute-start | bytes 1105928 | tf_op jit(solution)/shard_map/ppermute | solution.py:41
  22.7 17.4 %collective-permute-start.1 = (f32[72,1280]{1,0:T(8,128)S(1)}, f32[72,1280]{1,0:T(8,128)S(1)}, u32[]{:S(2)}, u32[]{:S(2)}) collective-permute-start(f32[72,1280]{1,0:T(8,128)S(1)} %maximum_maximum_fusion), channel_id=1, source_target_pairs={{0,32},{1,33},{2,34},{3,35},{4,36},{5,37},{6,38},{7,39},{8,40},{9,... | collective-permute-start | bytes 1105928 | tf_op jit(solution)/shard_map/ppermute | solution.py:41
  40.1 7.8 %copy-start.8 = (f32[72,1280]{1,0:T(8,128)}, f32[72,1280]{1,0:T(8,128)S(1)}, u32[]{:S(2)}) copy-start(f32[72,1280]{1,0:T(8,128)S(1)} %collective-permute-done.1) | copy-start | bytes 1105924
  41.9 26.8 %copy-start.5 = (bf16[64,1280]{1,0:T(8,128)(2,1)}, bf16[64,1280]{1,0:T(8,128)(2,1)S(1)}, u32[]{:S(2)}) copy-start(bf16[64,1280]{1,0:T(8,128)(2,1)S(1)} %get-tuple-element.13.refs_0_) | copy-start | bytes 491524
  42.0 10.5 %collective-permute-start.6 = (bf16[64,1280]{1,0:T(8,128)(2,1)S(1)}, bf16[64,1280]{1,0:T(8,128)(2,1)S(1)}, u32[]{:S(2)}, u32[]{:S(2)}) collective-permute-start(bf16[64,1280]{1,0:T(8,128)(2,1)S(1)} %get-tuple-element.13.refs_0_), channel_id=1, source_target_pairs={{0,128},{1,129},{2,130},{3,131},{4,132},{5,133},{6,134},{7,135},{8... | collective-permute-start | bytes 491528 | tf_op jit(solution)/shard_map/ppermute | solution.py:41
  47.9 10.4 %collective-permute-start.7 = (bf16[64,1280]{1,0:T(8,128)(2,1)S(1)}, bf16[64,1280]{1,0:T(8,128)(2,1)S(1)}, u32[]{:S(2)}, u32[]{:S(2)}) collective-permute-start(bf16[64,1280]{1,0:T(8,128)(2,1)S(1)} %get-tuple-element.13.refs_0_), channel_id=1, source_target_pairs={{0,64},{1,65},{2,66},{3,67},{4,68},{5,69},{6,70},{7,71},{8,72},{9,... | collective-permute-start | bytes 491528 | tf_op jit(solution)/shard_map/ppermute | solution.py:41
  49.6 9.9 %collective-permute-start.8 = (bf16[64,1280]{1,0:T(8,128)(2,1)S(1)}, bf16[64,1280]{1,0:T(8,128)(2,1)S(1)}, u32[]{:S(2)}, u32[]{:S(2)}) collective-permute-start(bf16[64,1280]{1,0:T(8,128)(2,1)S(1)} %get-tuple-element.13.refs_0_), channel_id=1, source_target_pairs={{0,192},{1,193},{2,194},{3,195},{4,196},{5,197},{6,198},{7,199},{8... | collective-permute-start | bytes 491528 | tf_op jit(solution)/shard_map/ppermute | solution.py:41
  52.5 16.3 %copy-start.9 = (bf16[64,1280]{1,0:T(8,128)(2,1)}, bf16[64,1280]{1,0:T(8,128)(2,1)S(1)}, u32[]{:S(2)}) copy-start(bf16[64,1280]{1,0:T(8,128)(2,1)S(1)} %collective-permute-done.6.refs_1_) | copy-start | bytes 491524
  58.3 10.5 %copy-start.10 = (bf16[64,1280]{1,0:T(8,128)(2,1)}, bf16[64,1280]{1,0:T(8,128)(2,1)S(1)}, u32[]{:S(2)}) copy-start(bf16[64,1280]{1,0:T(8,128)(2,1)S(1)} %collective-permute-done.7.refs_2_) | copy-start | bytes 491524
  59.5 9.3 %copy-start.11 = (bf16[64,1280]{1,0:T(8,128)(2,1)}, bf16[64,1280]{1,0:T(8,128)(2,1)S(1)}, u32[]{:S(2)}) copy-start(bf16[64,1280]{1,0:T(8,128)(2,1)S(1)} %collective-permute-done.8.refs_3_) | copy-start | bytes 491524
  59.5 8.6 %collective-permute-start.9 = (bf16[64,1280]{1,0:T(8,128)(2,1)S(1)}, bf16[64,1280]{1,0:T(8,128)(2,1)S(1)}, u32[]{:S(2)}, u32[]{:S(2)}) collective-permute-start(bf16[64,1280]{1,0:T(8,128)(2,1)S(1)} %get-tuple-element.13.refs_0_), channel_id=1, source_target_pairs={{0,144},{1,145},{2,146},{3,147},{4,148},{5,149},{6,150},{7,151},{8... | collective-permute-start | bytes 491528 | tf_op jit(solution)/shard_map/ppermute | solution.py:41
  59.7 8.5 %collective-permute-start.10 = (bf16[64,1280]{1,0:T(8,128)(2,1)S(1)}, bf16[64,1280]{1,0:T(8,128)(2,1)S(1)}, u32[]{:S(2)}, u32[]{:S(2)}) collective-permute-start(bf16[64,1280]{1,0:T(8,128)(2,1)S(1)} %get-tuple-element.13.refs_0_), channel_id=1, source_target_pairs={{0,80},{1,81},{2,82},{3,83},{4,84},{5,85},{6,86},{7,87},{8,88},{9,... | collective-permute-start | bytes 491528 | tf_op jit(solution)/shard_map/ppermute | solution.py:41
  63.1 5.4 %collective-permute-start.11 = (bf16[64,1280]{1,0:T(8,128)(2,1)S(1)}, bf16[64,1280]{1,0:T(8,128)(2,1)S(1)}, u32[]{:S(2)}, u32[]{:S(2)}) collective-permute-start(bf16[64,1280]{1,0:T(8,128)(2,1)S(1)} %get-tuple-element.13.refs_0_), channel_id=1, source_target_pairs={{0,208},{1,209},{2,210},{3,211},{4,212},{5,213},{6,214},{7,215},{8... | collective-permute-start | bytes 491528 | tf_op jit(solution)/shard_map/ppermute | solution.py:41
  63.1 5.7 %collective-permute-start.12 = (bf16[64,1280]{1,0:T(8,128)(2,1)S(1)}, bf16[64,1280]{1,0:T(8,128)(2,1)S(1)}, u32[]{:S(2)}, u32[]{:S(2)}) collective-permute-start(bf16[64,1280]{1,0:T(8,128)(2,1)S(1)} %get-tuple-element.13.refs_0_), channel_id=1, source_target_pairs={{0,16},{1,17},{2,18},{3,19},{4,20},{5,21},{6,22},{7,23},{8,24},{9,... | collective-permute-start | bytes 491528 | tf_op jit(solution)/shard_map/ppermute | solution.py:41
  68.1 0.7 copy-start.12
  68.1 0.7 copy-start.13
  69.2 0.7 copy-start.15
  85.4 9.2 %collective-permute-start.14 = (bf16[512,4096]{1,0:T(8,128)(2,1)}, bf16[512,4096]{1,0:T(8,128)(2,1)}, u32[]{:S(2)}, u32[]{:S(2)}) collective-permute-start(bf16[512,4096]{1,0:T(8,128)(2,1)} %get-tuple-element.17), channel_id=1, source_target_pairs={{0,32},{1,33},{2,34},{3,35},{4,36},{5,37},{6,38},{7,39},{8,40},{9,... | collective-permute-start | bytes 12582920 | tf_op jit(solution)/shard_map/ppermute | solution.py:41
  86.0 7.0 %collective-permute-start.13 = (f32[64,1280]{1,0:T(8,128)S(1)}, f32[64,1280]{1,0:T(8,128)S(1)}, u32[]{:S(2)}, u32[]{:S(2)}) collective-permute-start(f32[64,1280]{1,0:T(8,128)S(1)} %pad_maximum_fusion.5), channel_id=1, source_target_pairs={{0,32},{1,33},{2,34},{3,35},{4,36},{5,37},{6,38},{7,39},{8,40},{9,... | collective-permute-start | bytes 983048 | tf_op jit(solution)/shard_map/ppermute | solution.py:41
  139.2 3.4 %copy-start.2 = (bf16[1024,4096]{1,0:T(8,128)(2,1)S(1)}, bf16[1024,4096]{1,0:T(8,128)(2,1)}, u32[]{:S(2)}) copy-start(bf16[1024,4096]{1,0:T(8,128)(2,1)} %pad_maximum_fusion.rows) | copy-start | bytes 25165828
  156.1 5.5 %copy-start = (f32[1024,1280]{1,0:T(8,128)}, f32[1024,1280]{1,0:T(8,128)S(1)}, u32[]{:S(2)}) copy-start(f32[1024,1280]{1,0:T(8,128)S(1)} %project.1) | copy-start | bytes 15728644
  161.6 9.6 %collective-permute-start.15 = (bf16[512,1024]{1,0:T(8,128)(2,1)S(1)}, bf16[512,1024]{1,0:T(8,128)(2,1)S(1)}, u32[]{:S(2)}, u32[]{:S(2)}) collective-permute-start(bf16[512,1024]{1,0:T(8,128)(2,1)S(1)} %attend.2), channel_id=1, source_target_pairs={{0,32},{1,33},{2,34},{3,35},{4,36},{5,37},{6,38},{7,39},{8,40},{9,... | collective-permute-start | bytes 3145736 | tf_op jit(solution)/shard_map/ppermute | solution.py:41
  162.6 2.5 %copy-start.1 = (f32[1024,1280]{1,0:T(8,128)S(1)}, f32[1024,1280]{1,0:T(8,128)}, u32[]{:S(2)}) copy-start(f32[1024,1280]{1,0:T(8,128)} %copy-done) | copy-start | bytes 15728644
  171.2 1.0 copy-start.4
  (1 other events, 0.7 us)
Sparse Core Ops, SparseCore 0:
  73.2 65.9 all-gather.1

commit v3 on v2

--- a/solution.py
+++ b/solution.py
@@ -185,7 +185,7 @@
             pl.BlockSpec((D, tile), lambda n: (0, n)),
         ],
         out_specs=pl.BlockSpec((count, tile), lambda n: (0, n)),
-        compiler_params=pltpu.CompilerParams(vmem_limit_bytes=32 << 20),
+        compiler_params=pltpu.CompilerParams(vmem_limit_bytes=24 << 20),
         cost_estimate=pl.CostEstimate(
             flops=2 * count * D * width,
             transcendentals=0,
@@ -266,7 +266,7 @@
                 pltpu.VMEM((SEQ, HD), jnp.bfloat16),
             ],
         ),
-        compiler_params=pltpu.CompilerParams(vmem_limit_bytes=24 << 20),
+        compiler_params=pltpu.CompilerParams(vmem_limit_bytes=16 << 20),
         cost_estimate=pl.CostEstimate(
             flops=4 * SEQ * SEQ * width,
             transcendentals=SEQ * SEQ * width // HD,
@@ -295,7 +295,7 @@
             out_specs=pl.BlockSpec((SEQ, width), lambda j, at: (0, at[0] + j)),
         ),
         input_output_aliases={2: 0},
-        compiler_params=pltpu.CompilerParams(vmem_limit_bytes=VMEM_LIMIT),
+        compiler_params=pltpu.CompilerParams(vmem_limit_bytes=16 << 20),
         cost_estimate=pl.CostEstimate(
             flops=0, transcendentals=0, bytes_accessed=4 * SEQ * part.shape[1]
         ),

time: 182 us -> 183 us (level)
  local copies, waits for them, and re-layouts: 11.1 us -> 14.1 us
  Pallas kernels: 40.3 us -> 38.4 us
    unnamed x32, local copies, waits for them, and re-layouts: 7.94 us -> 10.9 us
where the time goes in v3:
time: 183 us; the launch traced here: 182 us
  waiting for transfers between devices  68.3 us (37%)
  Pallas kernels  38.4 us (21%)
  starting transfers between devices  27.2 us (15%)
  other arithmetic  18 us (10%)
  between operations  16.2 us (9%)
  local copies, waits for them, and re-layouts  14.1 us (8%)
    all_gather x1, waiting for transfers between devices, per_device(): lax.all_gather(whole, AXES, axis=0, tiled=True, axis_index_groups=far_gro...  36.5 us
    ppermute x16, waiting for transfers between devices, send(): return lax.ppermute(value, AXES, pairs(target))  31.7 us
    ppermute x16, starting transfers between devices, send(): return lax.ppermute(value, AXES, pairs(target))  27.2 us
    pallas_call x1, Pallas kernels, project(): pl.pallas_call(project_kernel, out_shape=jax.ShapeDtypeStruct((count, wid...  12.7 us
    pallas_call x2, Pallas kernels, attend(): pl.pallas_call(attend_kernel, out_shape=jax.ShapeDtypeStruct((SEQ, column...  11.6 us
    unnamed x32, local copies, waits for them, and re-layouts  10.9 us
    pallas_call x1, Pallas kernels, normalize(): pl.pallas_call(norm_kernel, out_shape=(shape, shape), grid_spec=pltpu.Pre...  9.9 us
    concatenate x1, other arithmetic, per_device(): normed = jnp.concatenate([kept, send(given, sibling)])  8.06 us
  transfers between devices with their start and end apart: 17, of which 11 were waited for; matrix products, arithmetic and copies ran while one was open for 10% of the time, Pallas kernels for 9%

profile of v3, /device:TPU:1, one launch (start us, length us, event | category | flops | bytes accessed | tf_op | source)
XLA Modules:
  0.0 182.2 jit_solution(4731498587220969425)
XLA Ops:
  7.9 1.5 multiply_bitcast_fusion
  9.4 1.2 concatenate.43
  10.5 3.2 %collective-permute-start = (f32[264,1280]{1,0:T(8,128)}, f32[264,1280]{1,0:T(8,128)}, u32[]{:S(2)}, u32[]{:S(2)}) collective-permute-start(f32[264,1280]{1,0:T(8,128)} %concatenate.43), channel_id=1, source_target_pairs={{0,32},{1,33},{2,34},{3,35},{4,36},{5,37},{6,38},{7,39},{8,40},{9,... | collective-permute-start | bytes 4055048 | tf_op jit(solution)/shard_map/ppermute | solution.py:41
  13.8 1.2 collective-permute-start.5
  16.8 1.5 slice_add_fusion
  19.4 1.8 collective-permute-start.4
  22.7 1.1 collective-permute-start.1
  23.9 7.1 %collective-permute-done.4 = f32[72,1280]{1,0:T(8,128)S(1)} collective-permute-done((f32[72,1280]{1,0:T(8,128)S(1)}, f32[72,1280]{1,0:T(8,128)S(1)}, u32[]{:S(2)}, u32[]{:S(2)}) %collective-permute-start.4) | collective-permute-done | bytes 368672 | tf_op jit(solution)/shard_map/ppermute | solution.py:41
  31.0 7.0 %collective-permute-done.3 = f32[72,1280]{1,0:T(8,128)S(1)} collective-permute-done((f32[72,1280]{1,0:T(8,128)S(1)}, f32[72,1280]{1,0:T(8,128)S(1)}, u32[]{:S(2)}, u32[]{:S(2)}) %collective-permute-start.3) | collective-permute-done | bytes 368672 | tf_op jit(solution)/shard_map/ppermute | solution.py:41
  38.0 1.5 collective-permute-done.2
  40.1 1.1 slice_select_fusion.9
  42.0 5.9 %collective-permute-start.6 = (bf16[64,1280]{1,0:T(8,128)(2,1)S(1)}, bf16[64,1280]{1,0:T(8,128)(2,1)S(1)}, u32[]{:S(2)}, u32[]{:S(2)}) collective-permute-start(bf16[64,1280]{1,0:T(8,128)(2,1)S(1)} %get-tuple-element.13.refs_0_), channel_id=1, source_target_pairs={{0,128},{1,129},{2,130},{3,131},{4,132},{5,133},{6,134},{7,135},{8... | collective-permute-start | bytes 491528 | tf_op jit(solution)/shard_map/ppermute | solution.py:41
  47.9 1.6 collective-permute-start.7
  49.6 2.8 %collective-permute-start.8 = (bf16[64,1280]{1,0:T(8,128)(2,1)S(1)}, bf16[64,1280]{1,0:T(8,128)(2,1)S(1)}, u32[]{:S(2)}, u32[]{:S(2)}) collective-permute-start(bf16[64,1280]{1,0:T(8,128)(2,1)S(1)} %get-tuple-element.13.refs_0_), channel_id=1, source_target_pairs={{0,192},{1,193},{2,194},{3,195},{4,196},{5,197},{6,198},{7,199},{8... | collective-permute-start | bytes 491528 | tf_op jit(solution)/shard_map/ppermute | solution.py:41
  52.5 5.8 %collective-permute-done.7.refs_2_ = bf16[64,1280]{1,0:T(8,128)(2,1)S(1)} collective-permute-done((bf16[64,1280]{1,0:T(8,128)(2,1)S(1)}, bf16[64,1280]{1,0:T(8,128)(2,1)S(1)}, u32[]{:S(2)}, u32[]{:S(2)}) %collective-permute-start.7) | collective-permute-done | bytes 163872 | tf_op jit(solution)/shard_map/ppermute | solution.py:41
  58.3 1.2 collective-permute-done.8.refs_3_
  59.7 3.4 %collective-permute-start.10 = (bf16[64,1280]{1,0:T(8,128)(2,1)S(1)}, bf16[64,1280]{1,0:T(8,128)(2,1)S(1)}, u32[]{:S(2)}, u32[]{:S(2)}) collective-permute-start(bf16[64,1280]{1,0:T(8,128)(2,1)S(1)} %get-tuple-element.13.refs_0_), channel_id=1, source_target_pairs={{0,80},{1,81},{2,82},{3,83},{4,84},{5,85},{6,86},{7,87},{8,88},{9,... | collective-permute-start | bytes 491528 | tf_op jit(solution)/shard_map/ppermute | solution.py:41
  63.1 2.7 %collective-permute-start.12 = (bf16[64,1280]{1,0:T(8,128)(2,1)S(1)}, bf16[64,1280]{1,0:T(8,128)(2,1)S(1)}, u32[]{:S(2)}, u32[]{:S(2)}) collective-permute-start(bf16[64,1280]{1,0:T(8,128)(2,1)S(1)} %get-tuple-element.13.refs_0_), channel_id=1, source_target_pairs={{0,16},{1,17},{2,18},{3,19},{4,20},{5,21},{6,22},{7,23},{8,24},{9,... | collective-permute-start | bytes 491528 | tf_op jit(solution)/shard_map/ppermute | solution.py:41
  66.3 1.8 %collective-permute-done.5.other = bf16[512,2048]{1,0:T(8,128)(2,1)} collective-permute-done((bf16[512,2048]{1,0:T(8,128)(2,1)}, bf16[512,2048]{1,0:T(8,128)(2,1)}, u32[]{:S(2)}, u32[]{:S(2)}) %collective-permute-start.5) | collective-permute-done | bytes 2097184 | tf_op jit(solution)/shard_map/ppermute | solution.py:41
  69.8 3.2 %place.1 = bf16[512,1280]{1,0:T(8,128)(2,1)} custom-call(s32[8]{0:T(128)} %broadcast_multiply_fusion.at_ref, bf16[64,1280]{1,0:T(8,128)(2,1)} %copy-done.5, bf16[64,1280]{1,0:T(8,128)(2,1)} %copy-done.9, bf16[64,1280]{1,0:T(8,128)(2,1)} %copy-done.10, bf16[64,1280]{1,0:T(8,128)(2,1)} %copy-done.11, bf16[64,1280]{1,0:T(8,128)(2,1)} %copy-done.12, ...), custom_call_target="tpu_custom_call" | custom-call | bytes 2621440 | tf_op jit(solution)/shard_map/place/pallas_call | solution.py:101
  73.1 1.2 slice.72
  75.5 9.9 %normalize.1 = (bf16[512,4096]{1,0:T(8,128)(2,1)}, bf16[512,4096]{1,0:T(8,128)(2,1)}) custom-call(s32[2]{0:T(128)} %get-tuple-element.45.where_ref, bf16[512,2048]{1,0:T(8,128)(2,1)} %bitcast.18.own, bf16[512,2048]{1,0:T(8,128)(2,1)} %collective-permute-done.5.other, f32[1,4096]{1,0:T(1,128)} %bitcast.39), custom_call_target="tpu_custom_call" | custom-call | flops 16777216 | bytes 12582912 | tf_op jit(solution)/shard_map/normalize/pallas_call | solution.py:155
  87.5 5.6 %collective-permute-done.13 = f32[64,1280]{1,0:T(8,128)S(1)} collective-permute-done((f32[64,1280]{1,0:T(8,128)S(1)}, f32[64,1280]{1,0:T(8,128)S(1)}, u32[]{:S(2)}, u32[]{:S(2)}) %collective-permute-start.13) | collective-permute-done | bytes 327712 | tf_op jit(solution)/shard_map/ppermute | solution.py:41
  94.6 8.1 %pad_maximum_fusion.rows = bf16[1024,4096]{1,0:T(8,128)(2,1)} fusion(bf16[512,4096]{1,0:T(8,128)(2,1)} %collective-permute-done.14, bf16[512,4096]{1,0:T(8,128)(2,1)} %get-tuple-element.16), kind=kLoop, calls=%fused_computation | loop fusion | flops 16777216 | bytes 16777216 | tf_op jit(solution)/shard_map/concatenate | solution.py:397
  102.7 36.5 %all-gather.2.cloned.1.call-done.weights = bf16[4096,1280]{1,0:T(8,128)(2,1)} async-done(((bf16[512,1280]{1,0:T(8,128)(2,1)}), bf16[4096,1280]{1,0:T(8,128)(2,1)}) %all-gather.2.cloned.1.call-update) | async-done | bytes 10485776 | tf_op jit(solution)/shard_map/all_gather | solution.py:394
  139.2 3.4 %copy-done.2 = bf16[1024,4096]{1,0:T(8,128)(2,1)S(1)} copy-done((bf16[1024,4096]{1,0:T(8,128)(2,1)S(1)}, bf16[1024,4096]{1,0:T(8,128)(2,1)}, u32[]{:S(2)}) %copy-start.2) | copy-done | bytes 8388632
  142.6 4.0 %copy-done.3 = bf16[4096,1280]{1,0:T(8,128)(2,1)S(1)} copy-done((bf16[4096,1280]{1,0:T(8,128)(2,1)S(1)}, bf16[4096,1280]{1,0:T(8,128)(2,1)}, u32[]{:S(2)}) %copy-start.3) | copy-done | bytes 10485784
  146.5 12.7 %project.1 = f32[1024,1280]{1,0:T(8,128)S(1)} custom-call(bf16[1024,4096]{1,0:T(8,128)(2,1)S(1)} %copy-done.2, bf16[4096,1280]{1,0:T(8,128)(2,1)S(1)} %copy-done.3), custom_call_target="tpu_custom_call" | custom-call | flops 10737418240 | bytes 24117248 | tf_op jit(solution)/shard_map/project/pallas_call | solution.py:179
  159.2 5.5 %attend.2 = bf16[512,1024]{1,0:T(8,128)(2,1)S(1)} custom-call(s32[2]{0:T(128)S(1)} %get-tuple-element.44.at_ref, f32[2,512,1280]{2,1,0:T(8,128)S(1)} %bitcast.33, f32[2,512,1280]{2,1,0:T(8,128)S(1)} %bitcast.34, f32[512,128]{1,0:T(8,128)S(1)} %get-tuple-element.48.cos_ref, f32[512,128]{1,0:T(8,128)S(1)} %get-tuple-element.49.sin_ref), custom_call_target="tpu_custom_call" | custom-call | flops 1073741824 | bytes 3145728 | tf_op jit(solution)/shard_map/attend/pallas_call | solution.py:251
  165.7 2.5 %copy-done.1 = f32[1024,1280]{1,0:T(8,128)S(1)} copy-done((f32[1024,1280]{1,0:T(8,128)S(1)}, f32[1024,1280]{1,0:T(8,128)}, u32[]{:S(2)}) %copy-start.1) | copy-done | bytes 5242904
  168.2 6.1 %attend.3._ = bf16[512,2048]{1,0:T(8,128)(2,1)} custom-call(s32[2]{0:T(128)S(1)} %pad_add_fusion.2.at_ref, f32[2,512,1280]{2,1,0:T(8,128)S(1)} %bitcast.35, f32[2,512,1280]{2,1,0:T(8,128)S(1)} %bitcast.36, f32[512,128]{1,0:T(8,128)S(1)} %get-tuple-element.48.cos_ref, f32[512,128]{1,0:T(8,128)S(1)} %get-tuple-element.49.sin_ref), custom_call_target="tpu_custom_call" | custom-call | flops 1073741824 | bytes 3145728 | tf_op jit(solution)/shard_map/attend/pallas_call | solution.py:251
  174.3 1.1 insert.1
  (70 shorter events, 12.9 us)
Async XLA Ops:
  7.2 132.0 %all-gather.2.cloned.1.call-start = ((), (), s32[]{:S(2)}) async-start(), calls=%async_computation | async-start | bytes 11796480 | tf_op jit(solution)/shard_map/all_gather | solution.py:394
  7.9 7.8 %copy-start.6 = (f32[32,2560]{1,0:T(8,128)S(1)}, f32[32,2560]{1,0:T(8,128)}, u32[]{:S(2)}) copy-start(f32[32,2560]{1,0:T(8,128)} %param.10) | copy-start | bytes 983044
  9.3 6.4 %copy-start.7 = (f32[32,2560]{1,0:T(8,128)S(1)}, f32[32,2560]{1,0:T(8,128)}, u32[]{:S(2)}) copy-start(f32[32,2560]{1,0:T(8,128)} %param.9) | copy-start | bytes 983044
  9.4 7.5 %copy-start.4 = (f32[1,256,2560]{2,1,0:T(8,128)S(1)}, f32[1,256,2560]{2,1,0:T(8,128)}, u32[]{:S(2)}) copy-start(f32[1,256,2560]{2,1,0:T(8,128)} %param.7) | copy-start | bytes 7864324
  10.5 6.3 %collective-permute-start = (f32[264,1280]{1,0:T(8,128)}, f32[264,1280]{1,0:T(8,128)}, u32[]{:S(2)}, u32[]{:S(2)}) collective-permute-start(f32[264,1280]{1,0:T(8,128)} %concatenate.43), channel_id=1, source_target_pairs={{0,32},{1,33},{2,34},{3,35},{4,36},{5,37},{6,38},{7,39},{8,40},{9,... | collective-permute-start | bytes 4055048 | tf_op jit(solution)/shard_map/ppermute | solution.py:41
  13.8 54.3 %collective-permute-start.5 = (bf16[512,2048]{1,0:T(8,128)(2,1)}, bf16[512,2048]{1,0:T(8,128)(2,1)}, u32[]{:S(2)}, u32[]{:S(2)}) collective-permute-start(bf16[512,2048]{1,0:T(8,128)(2,1)} %bitcast.18.own), channel_id=1, source_target_pairs={{0,1},{1,0},{2,3},{3,2},{4,5},{5,4},{6,7},{7,6},{8,9},{9,8},{10,11... | collective-permute-start | bytes 6291464 | tf_op jit(solution)/shard_map/ppermute | solution.py:41
  19.4 11.6 %collective-permute-start.4 = (f32[72,1280]{1,0:T(8,128)S(1)}, f32[72,1280]{1,0:T(8,128)S(1)}, u32[]{:S(2)}, u32[]{:S(2)}) collective-permute-start(f32[72,1280]{1,0:T(8,128)S(1)} %get-tuple-element.40), channel_id=1, source_target_pairs={{0,128},{1,129},{2,130},{3,131},{4,132},{5,133},{6,134},{7,135},{8... | collective-permute-start | bytes 1105928 | tf_op jit(solution)/shard_map/ppermute | solution.py:41
  21.1 16.9 %collective-permute-start.3 = (f32[72,1280]{1,0:T(8,128)S(1)}, f32[72,1280]{1,0:T(8,128)S(1)}, u32[]{:S(2)}, u32[]{:S(2)}) collective-permute-start(f32[72,1280]{1,0:T(8,128)S(1)} %get-tuple-element.39), channel_id=1, source_target_pairs={{0,192},{1,193},{2,194},{3,195},{4,196},{5,197},{6,198},{7,199},{8... | collective-permute-start | bytes 1105928 | tf_op jit(solution)/shard_map/ppermute | solution.py:41
  22.0 17.5 %collective-permute-start.2 = (f32[72,1280]{1,0:T(8,128)S(1)}, f32[72,1280]{1,0:T(8,128)S(1)}, u32[]{:S(2)}, u32[]{:S(2)}) collective-permute-start(f32[72,1280]{1,0:T(8,128)S(1)} %get-tuple-element.38), channel_id=1, source_target_pairs={{0,64},{1,65},{2,66},{3,67},{4,68},{5,69},{6,70},{7,71},{8,72},{9,... | collective-permute-start | bytes 1105928 | tf_op jit(solution)/shard_map/ppermute | solution.py:41
  22.7 17.4 %collective-permute-start.1 = (f32[72,1280]{1,0:T(8,128)S(1)}, f32[72,1280]{1,0:T(8,128)S(1)}, u32[]{:S(2)}, u32[]{:S(2)}) collective-permute-start(f32[72,1280]{1,0:T(8,128)S(1)} %maximum_maximum_fusion), channel_id=1, source_target_pairs={{0,32},{1,33},{2,34},{3,35},{4,36},{5,37},{6,38},{7,39},{8,40},{9,... | collective-permute-start | bytes 1105928 | tf_op jit(solution)/shard_map/ppermute | solution.py:41
  40.1 7.8 %copy-start.8 = (f32[72,1280]{1,0:T(8,128)}, f32[72,1280]{1,0:T(8,128)S(1)}, u32[]{:S(2)}) copy-start(f32[72,1280]{1,0:T(8,128)S(1)} %collective-permute-done.1) | copy-start | bytes 1105924
  41.9 26.8 %copy-start.5 = (bf16[64,1280]{1,0:T(8,128)(2,1)}, bf16[64,1280]{1,0:T(8,128)(2,1)S(1)}, u32[]{:S(2)}) copy-start(bf16[64,1280]{1,0:T(8,128)(2,1)S(1)} %get-tuple-element.13.refs_0_) | copy-start | bytes 491524
  42.0 10.5 %collective-permute-start.6 = (bf16[64,1280]{1,0:T(8,128)(2,1)S(1)}, bf16[64,1280]{1,0:T(8,128)(2,1)S(1)}, u32[]{:S(2)}, u32[]{:S(2)}) collective-permute-start(bf16[64,1280]{1,0:T(8,128)(2,1)S(1)} %get-tuple-element.13.refs_0_), channel_id=1, source_target_pairs={{0,128},{1,129},{2,130},{3,131},{4,132},{5,133},{6,134},{7,135},{8... | collective-permute-start | bytes 491528 | tf_op jit(solution)/shard_map/ppermute | solution.py:41
  47.9 10.4 %collective-permute-start.7 = (bf16[64,1280]{1,0:T(8,128)(2,1)S(1)}, bf16[64,1280]{1,0:T(8,128)(2,1)S(1)}, u32[]{:S(2)}, u32[]{:S(2)}) collective-permute-start(bf16[64,1280]{1,0:T(8,128)(2,1)S(1)} %get-tuple-element.13.refs_0_), channel_id=1, source_target_pairs={{0,64},{1,65},{2,66},{3,67},{4,68},{5,69},{6,70},{7,71},{8,72},{9,... | collective-permute-start | bytes 491528 | tf_op jit(solution)/shard_map/ppermute | solution.py:41
  49.6 9.9 %collective-permute-start.8 = (bf16[64,1280]{1,0:T(8,128)(2,1)S(1)}, bf16[64,1280]{1,0:T(8,128)(2,1)S(1)}, u32[]{:S(2)}, u32[]{:S(2)}) collective-permute-start(bf16[64,1280]{1,0:T(8,128)(2,1)S(1)} %get-tuple-element.13.refs_0_), channel_id=1, source_target_pairs={{0,192},{1,193},{2,194},{3,195},{4,196},{5,197},{6,198},{7,199},{8... | collective-permute-start | bytes 491528 | tf_op jit(solution)/shard_map/ppermute | solution.py:41
  52.5 16.3 %copy-start.9 = (bf16[64,1280]{1,0:T(8,128)(2,1)}, bf16[64,1280]{1,0:T(8,128)(2,1)S(1)}, u32[]{:S(2)}) copy-start(bf16[64,1280]{1,0:T(8,128)(2,1)S(1)} %collective-permute-done.6.refs_1_) | copy-start | bytes 491524
  58.3 10.5 %copy-start.10 = (bf16[64,1280]{1,0:T(8,128)(2,1)}, bf16[64,1280]{1,0:T(8,128)(2,1)S(1)}, u32[]{:S(2)}) copy-start(bf16[64,1280]{1,0:T(8,128)(2,1)S(1)} %collective-permute-done.7.refs_2_) | copy-start | bytes 491524
  59.5 9.3 %copy-start.11 = (bf16[64,1280]{1,0:T(8,128)(2,1)}, bf16[64,1280]{1,0:T(8,128)(2,1)S(1)}, u32[]{:S(2)}) copy-start(bf16[64,1280]{1,0:T(8,128)(2,1)S(1)} %collective-permute-done.8.refs_3_) | copy-start | bytes 491524
  59.5 8.6 %collective-permute-start.9 = (bf16[64,1280]{1,0:T(8,128)(2,1)S(1)}, bf16[64,1280]{1,0:T(8,128)(2,1)S(1)}, u32[]{:S(2)}, u32[]{:S(2)}) collective-permute-start(bf16[64,1280]{1,0:T(8,128)(2,1)S(1)} %get-tuple-element.13.refs_0_), channel_id=1, source_target_pairs={{0,144},{1,145},{2,146},{3,147},{4,148},{5,149},{6,150},{7,151},{8... | collective-permute-start | bytes 491528 | tf_op jit(solution)/shard_map/ppermute | solution.py:41
  59.7 8.5 %collective-permute-start.10 = (bf16[64,1280]{1,0:T(8,128)(2,1)S(1)}, bf16[64,1280]{1,0:T(8,128)(2,1)S(1)}, u32[]{:S(2)}, u32[]{:S(2)}) collective-permute-start(bf16[64,1280]{1,0:T(8,128)(2,1)S(1)} %get-tuple-element.13.refs_0_), channel_id=1, source_target_pairs={{0,80},{1,81},{2,82},{3,83},{4,84},{5,85},{6,86},{7,87},{8,88},{9,... | collective-permute-start | bytes 491528 | tf_op jit(solution)/shard_map/ppermute | solution.py:41
  63.1 5.4 %collective-permute-start.11 = (bf16[64,1280]{1,0:T(8,128)(2,1)S(1)}, bf16[64,1280]{1,0:T(8,128)(2,1)S(1)}, u32[]{:S(2)}, u32[]{:S(2)}) collective-permute-start(bf16[64,1280]{1,0:T(8,128)(2,1)S(1)} %get-tuple-element.13.refs_0_), channel_id=1, source_target_pairs={{0,208},{1,209},{2,210},{3,211},{4,212},{5,213},{6,214},{7,215},{8... | collective-permute-start | bytes 491528 | tf_op jit(solution)/shard_map/ppermute | solution.py:41
  63.1 5.7 %collective-permute-start.12 = (bf16[64,1280]{1,0:T(8,128)(2,1)S(1)}, bf16[64,1280]{1,0:T(8,128)(2,1)S(1)}, u32[]{:S(2)}, u32[]{:S(2)}) collective-permute-start(bf16[64,1280]{1,0:T(8,128)(2,1)S(1)} %get-tuple-element.13.refs_0_), channel_id=1, source_target_pairs={{0,16},{1,17},{2,18},{3,19},{4,20},{5,21},{6,22},{7,23},{8,24},{9,... | collective-permute-start | bytes 491528 | tf_op jit(solution)/shard_map/ppermute | solution.py:41
  68.1 0.7 copy-start.12
  68.1 0.7 copy-start.13
  69.2 0.7 copy-start.15
  85.4 9.2 %collective-permute-start.14 = (bf16[512,4096]{1,0:T(8,128)(2,1)}, bf16[512,4096]{1,0:T(8,128)(2,1)}, u32[]{:S(2)}, u32[]{:S(2)}) collective-permute-start(bf16[512,4096]{1,0:T(8,128)(2,1)} %get-tuple-element.17), channel_id=1, source_target_pairs={{0,32},{1,33},{2,34},{3,35},{4,36},{5,37},{6,38},{7,39},{8,40},{9,... | collective-permute-start | bytes 12582920 | tf_op jit(solution)/shard_map/ppermute | solution.py:41
  86.0 7.0 %collective-permute-start.13 = (f32[64,1280]{1,0:T(8,128)S(1)}, f32[64,1280]{1,0:T(8,128)S(1)}, u32[]{:S(2)}, u32[]{:S(2)}) collective-permute-start(f32[64,1280]{1,0:T(8,128)S(1)} %pad_maximum_fusion.5), channel_id=1, source_target_pairs={{0,32},{1,33},{2,34},{3,35},{4,36},{5,37},{6,38},{7,39},{8,40},{9,... | collective-permute-start | bytes 983048 | tf_op jit(solution)/shard_map/ppermute | solution.py:41
  139.2 3.4 %copy-start.2 = (bf16[1024,4096]{1,0:T(8,128)(2,1)S(1)}, bf16[1024,4096]{1,0:T(8,128)(2,1)}, u32[]{:S(2)}) copy-start(bf16[1024,4096]{1,0:T(8,128)(2,1)} %pad_maximum_fusion.rows) | copy-start | bytes 25165828
  142.6 4.0 %copy-start.3 = (bf16[4096,1280]{1,0:T(8,128)(2,1)S(1)}, bf16[4096,1280]{1,0:T(8,128)(2,1)}, u32[]{:S(2)}) copy-start(bf16[4096,1280]{1,0:T(8,128)(2,1)} %all-gather.2.cloned.1.call-done.weights) | copy-start | bytes 31457284
  159.2 5.5 %copy-start = (f32[1024,1280]{1,0:T(8,128)}, f32[1024,1280]{1,0:T(8,128)S(1)}, u32[]{:S(2)}) copy-start(f32[1024,1280]{1,0:T(8,128)S(1)} %project.1) | copy-start | bytes 15728644
  164.7 9.6 %collective-permute-start.15 = (bf16[512,1024]{1,0:T(8,128)(2,1)S(1)}, bf16[512,1024]{1,0:T(8,128)(2,1)S(1)}, u32[]{:S(2)}, u32[]{:S(2)}) collective-permute-start(bf16[512,1024]{1,0:T(8,128)(2,1)S(1)} %attend.2), channel_id=1, source_target_pairs={{0,32},{1,33},{2,34},{3,35},{4,36},{5,37},{6,38},{7,39},{8,40},{9,... | collective-permute-start | bytes 3145736 | tf_op jit(solution)/shard_map/ppermute | solution.py:41
  165.7 2.5 %copy-start.1 = (f32[1024,1280]{1,0:T(8,128)S(1)}, f32[1024,1280]{1,0:T(8,128)}, u32[]{:S(2)}) copy-start(f32[1024,1280]{1,0:T(8,128)} %copy-done) | copy-start | bytes 15728644
  (1 other events, 0.7 us)
Sparse Core Ops, SparseCore 0:
  73.2 65.9 all-gather.1
